TPU v7x, 32 devices: a whole 2x2x4 slice. The times are simulated.
32 devices in a mesh: row: 2 (over y), col: 16 (over z, x, core).
Axes of the slice: x: 2, y: 2, z: 4, core: 2. Of those that a mesh axis runs over, the one named last changes fastest.
Arguments:
- queries: bfloat16 [4096, 256], P(('row', 'col')), may hold values from -6 to 6
- keys: bfloat16 [4096, 256], P('col', 'row'), may hold values from -6 to 6
- values: bfloat16 [4096, 256], P('col', 'row'), may hold values from -0.59765625 to 0.59765625
- outputs: bfloat16 [4096, 256], P(('row', 'col')), may hold values from -0.59765625 to 0.59765625
- d_out: bfloat16 [4096, 256], P(('row', 'col')), may hold values from -6 to 6
- lse: float32 [2, 4096], P(None, ('row', 'col')), may hold values from 4 to 6
Outputs:
- d_queries: bfloat16 [4096, 256], P(('row', 'col'))
- d_keys: bfloat16 [4096, 256], P('col', 'row')
- d_values: bfloat16 [4096, 256], P('col', 'row')
All inputs are finite; a program needn't handle non-finite values.
Results may differ from a plain program's by a relative error of at most 0.0049.
Values may be sent and summed in bfloat16 or wider, within the bound.
A program may use at most 64 MiB of HBM per device.

v0:
```python
import jax
import jax.numpy as jnp
from jax import lax
from jax.sharding import PartitionSpec as P


def block_size(row_total):
    block_rows = row_total
    while block_rows > 512 and block_rows % 2 == 0:
        block_rows = block_rows // 2
    return block_rows


def head_slice(matrix, head_index, head_dim):
    return matrix[:, head_index * head_dim : (head_index + 1) * head_dim]


def contract_rows(left, right):
    return lax.dot_general(
        left, right, (((0,), (0,)), ((), ())), preferred_element_type=jnp.float32
    )


def score_terms(query_head, grad_head, lse_row, delta_row, key_head, value_head, scaling):
    scores = jnp.dot(query_head, key_head.T, preferred_element_type=jnp.float32)
    probs = jnp.exp(scores * scaling - lse_row[:, None])
    probs_low = probs.astype(jnp.bfloat16)
    grad_probs = jnp.dot(grad_head, value_head.T, preferred_element_type=jnp.float32)
    grad_scores = (probs * (grad_probs - delta_row[:, None])).astype(jnp.bfloat16)
    return (probs_low, grad_scores)


def block_grads(query_rows, grad_rows, lse_rows, delta_rows, key_all, value_all, head_dim):
    head_total = lse_rows.shape[0]
    scaling = head_dim ** (-0.5)
    key_terms = []
    value_terms = []
    for head_index in range(head_total):
        query_head = head_slice(query_rows, head_index, head_dim)
        grad_head = head_slice(grad_rows, head_index, head_dim)
        key_head = head_slice(key_all, head_index, head_dim)
        value_head = head_slice(value_all, head_index, head_dim)
        probs_low, grad_scores = score_terms(
            query_head,
            grad_head,
            lse_rows[head_index],
            delta_rows[head_index],
            key_head,
            value_head,
            scaling,
        )
        value_terms.append(contract_rows(probs_low, grad_head))
        key_terms.append(contract_rows(grad_scores, query_head))
    key_term = jnp.concatenate(key_terms, axis=1)
    value_term = jnp.concatenate(value_terms, axis=1)
    query_term = None
    return (key_term, value_term, query_term)


def split_blocks(query_all, grad_all, lse_all, delta_all):
    row_total, features = query_all.shape
    block_rows = block_size(row_total)
    steps_total = row_total // block_rows
    head_total = lse_all.shape[0]
    query_blocks = query_all.reshape(steps_total, block_rows, features)
    grad_blocks = grad_all.reshape(steps_total, block_rows, features)
    lse_blocks = lse_all.reshape(head_total, steps_total, block_rows).transpose(1, 0, 2)
    delta_blocks = delta_all.reshape(head_total, steps_total, block_rows).transpose(1, 0, 2)
    return (query_blocks, grad_blocks, lse_blocks, delta_blocks)


def query_pass(query_all, grad_all, lse_all, delta_all, key_all, value_all, head_dim):
    row_total, features = query_all.shape
    block_inputs = split_blocks(query_all, grad_all, lse_all, delta_all)
    empty_sums = jnp.zeros((key_all.shape[0], features), jnp.float32)

    def advance(running, inputs):
        key_sum, value_sum = running
        query_rows, grad_rows, lse_rows, delta_rows = inputs
        key_term, value_term, query_term = block_grads(
            query_rows, grad_rows, lse_rows, delta_rows, key_all, value_all, head_dim
        )
        return ((key_sum + key_term, value_sum + value_term), query_term)

    (key_sum, value_sum), query_terms = lax.scan(advance, (empty_sums, empty_sums), block_inputs)
    return (key_sum, value_sum, query_terms)


def query_only(query_rows, grad_rows, lse_rows, delta_rows, key_all, value_all, head_dim):
    row_total, features = query_rows.shape
    head_total = lse_rows.shape[0]
    scaling = head_dim ** (-0.5)
    block_inputs = split_blocks(query_rows, grad_rows, lse_rows, delta_rows)

    def one_block(inputs):
        query_part, grad_part, lse_part, delta_part = inputs
        pieces = []
        for head_index in range(head_total):
            query_head = head_slice(query_part, head_index, head_dim)
            grad_head = head_slice(grad_part, head_index, head_dim)
            key_head = head_slice(key_all, head_index, head_dim)
            value_head = head_slice(value_all, head_index, head_dim)
            probs_low, grad_scores = score_terms(
                query_head,
                grad_head,
                lse_part[head_index],
                delta_part[head_index],
                key_head,
                value_head,
                scaling,
            )
            pieces.append(jnp.dot(grad_scores, key_head, preferred_element_type=jnp.float32))
        return jnp.concatenate(pieces, axis=1)

    return lax.map(one_block, block_inputs).reshape(row_total, features)


def head_delta(d_out, outputs, head_total, head_dim):
    product = d_out.astype(jnp.float32) * outputs.astype(jnp.float32)
    return jnp.sum(product.reshape(product.shape[0], head_total, head_dim), axis=2).T


def per_device(queries, keys, values, outputs, d_out, lse):
    head_total = lse.shape[0]
    head_dim = queries.shape[1] // head_total
    scaling = head_dim ** (-0.5)
    delta = head_delta(d_out, outputs, head_total, head_dim)
    key_all, value_all = (
        lax.all_gather(keys, "row", axis=1, tiled=True),
        lax.all_gather(values, "row", axis=1, tiled=True),
    )
    query_all, grad_all = (
        lax.all_gather(queries, "col", axis=0, tiled=True),
        lax.all_gather(d_out, "col", axis=0, tiled=True),
    )
    lse_all, delta_all = (
        lax.all_gather(lse, "col", axis=1, tiled=True),
        lax.all_gather(delta, "col", axis=1, tiled=True),
    )
    key_sum, value_sum, unused_terms = query_pass(
        query_all, grad_all, lse_all, delta_all, key_all, value_all, head_dim
    )

    def query_term(first_row, row_total):
        return query_only(query_all, grad_all, lse_all, delta_all, key_all, value_all, head_dim)

    query_grad = lax.psum_scatter(
        query_term(jnp.int32(0), queries.shape[0] * lax.axis_size("col")),
        "col",
        scatter_dimension=0,
        tiled=True,
    )
    key_grad, value_grad = (
        lax.psum_scatter(key_sum, "row", scatter_dimension=1, tiled=True),
        lax.psum_scatter(value_sum, "row", scatter_dimension=1, tiled=True),
    )
    d_queries = (query_grad * scaling).astype(jnp.bfloat16)
    d_keys = (key_grad * scaling).astype(jnp.bfloat16)
    d_values = value_grad.astype(jnp.bfloat16)
    return (d_queries, d_keys, d_values)


def solution(mesh):
    placed = (
        P(("row", "col"), None),
        P("col", "row"),
        P("col", "row"),
        P(("row", "col"), None),
        P(("row", "col"), None),
        P(None, ("row", "col")),
    )
    return jax.shard_map(
        per_device,
        mesh=mesh,
        in_specs=placed,
        out_specs=(P(("row", "col"), None), P("col", "row"), P("col", "row")),
        check_vma=False,
    )
```

profile of v0, /device:TPU:0, one launch (start us, length us, event | category | flops | bytes accessed | tf_op | source)
XLA Modules:
  0.0 205.7 jit_solution(12299479593922273519)
XLA Ops:
  7.2 0.7 all-gather.3.cloned.1.call-update
  8.0 0.7 all-gather.5.cloned.1.call-update
  8.7 0.9 convert_multiply_fusion
  9.9 26.3 %all_gather.23 = f32[2,2048]{0,1:T(8,128)S(1)} all-gather(f32[2,128]{0,1:T(8,128)S(1)} %bitcast.55), channel_id=1, replica_groups=mesh['row'=2,'col'=16] {'col'}, dimensions={1}, use_global_device_ids=true | all-gather | bytes 17408 | tf_op jit(solution)/shard_map/all_gather | solution.py:138
  36.5 17.5 %all_gather.20 = f32[2,2048]{1,0:T(2,128)S(1)} all-gather(f32[2,128]{1,0:T(2,128)S(1)} %copy-done.2), channel_id=1, replica_groups=mesh['row'=2,'col'=16] {'col'}, dimensions={1}, use_global_device_ids=true | all-gather | bytes 17408 | tf_op jit(solution)/shard_map/all_gather | solution.py:137
  54.0 5.0 %all_gather.19 = bf16[256,256]{1,0:T(8,128)(2,1)S(1)} all-gather(bf16[256,128]{1,0:T(8,128)(2,1)S(1)} %copy-done), channel_id=1, replica_groups=mesh['row'=2,'col'=16] {'row'}, dimensions={1}, use_global_device_ids=true | all-gather | bytes 196608 | tf_op jit(solution)/shard_map/all_gather | solution.py:129
  59.0 5.0 %all_gather.22 = bf16[256,256]{1,0:T(8,128)(2,1)S(1)} all-gather(bf16[256,128]{1,0:T(8,128)(2,1)S(1)} %copy-done.1), channel_id=1, replica_groups=mesh['row'=2,'col'=16] {'row'}, dimensions={1}, use_global_device_ids=true | all-gather | bytes 196608 | tf_op jit(solution)/shard_map/all_gather | solution.py:130
  64.0 26.8 %all-gather.5.cloned.1.call-done = bf16[2048,256]{1,0:T(8,128)(2,1)} async-done(((bf16[128,256]{1,0:T(8,128)(2,1)}), bf16[2048,256]{1,0:T(8,128)(2,1)}) %all-gather.5.cloned.1.call-update) | async-done | bytes 1048592 | tf_op jit(solution)/shard_map/all_gather | solution.py:134
  90.8 16.1 %while.24 = (s32[]{:T(128)}, f32[256,256]{0,1:T(8,128)S(1)}, f32[256,256]{0,1:T(8,128)S(1)}, bf16[4,512,256]{2,1,0:T(8,128)(2,1)}, bf16[256,256]{1,0:T(8,128)(2,...) while((s32[]{:T(128)}, f32[256,256]{0,1:T(8,128)S(1)}, ...), condition=%wide.region_5.6_spmd.clone, body=%wide.region_4.5_spmd.clone.sunk | while | flops 270401536 | bytes 7626923 | solution.py:85
  90.8 1.0 dynamic-slice_bitcast_fusion.8
  92.1 1.0 dynamic-slice_bitcast_fusion.9
  93.0 0.4 fusion.119
  93.7 0.4 fusion.121
  94.9 1.0 dynamic-slice_bitcast_fusion.8
  96.1 1.0 dynamic-slice_bitcast_fusion.9
  97.1 0.4 fusion.119
  97.8 0.4 fusion.121
  98.9 1.0 dynamic-slice_bitcast_fusion.8
  100.2 1.0 dynamic-slice_bitcast_fusion.9
  101.1 0.4 fusion.119
  101.8 0.4 fusion.121
  102.9 1.0 dynamic-slice_bitcast_fusion.8
  104.2 1.0 dynamic-slice_bitcast_fusion.9
  105.9 0.4 fusion.121
  107.0 0.8 copy.22
  107.9 0.8 copy.21
  108.8 14.3 %while.23 = (s32[]{:T(128)}, f32[4,512,256]{2,1,0:T(8,128)}, bf16[4,512,256]{2,1,0:T(8,128)(2,1)}, bf16[256,256]{1,0:T(8,128)(2,1)S(1)}, f32[4,2,512]{2,1,0:T(2,...) while((s32[]{:T(128)}, f32[4,512,256]{2,1,0:T(8,128)}, ...), condition=%wide.region_2.3_spmd, body=%wide.region_1.2_spmd.sunk | while | flops 202768384 | bytes 7757969 | solution.py:115
  108.8 1.1 dynamic-slice_bitcast_fusion.7
  110.1 0.4 fusion.102
  110.8 0.4 fusion.103
  111.5 0.8 constant_dynamic-update-slice_fusion.2
  112.4 1.1 dynamic-slice_bitcast_fusion.7
  113.7 0.4 fusion.102
  114.4 0.4 fusion.103
  115.1 0.8 constant_dynamic-update-slice_fusion.2
  115.9 1.1 dynamic-slice_bitcast_fusion.7
  117.3 0.4 fusion.102
  117.9 0.4 fusion.103
  118.6 0.9 constant_dynamic-update-slice_fusion.2
  119.5 1.1 dynamic-slice_bitcast_fusion.7
  120.8 0.4 fusion.102
  121.5 0.4 fusion.103
  122.2 0.8 constant_dynamic-update-slice_fusion.2
  123.1 1.5 convert_element_type.37
  124.7 7.8 %reduce-scatter.6.cloned.1.call-done = f32[256,128]{1,0:T(8,128)} async-done(((f32[256,256]{1,0:T(8,128)}), f32[256,128]{1,0:T(8,128)}) %reduce-scatter.6.cloned.1.call-update) | async-done | bytes 131088 | tf_op jit(solution)/shard_map/reduce_scatter | solution.py:154
  132.4 1.5 multiply_convert_fusion
  134.0 63.6 %reduce-scatter.4.cloned.1.call-done = f32[128,256]{1,0:T(8,128)} async-done(((f32[2048,256]{1,0:T(8,128)}), f32[128,256]{1,0:T(8,128)}) %reduce-scatter.4.cloned.1.call-update) | async-done | bytes 131088 | tf_op jit(solution)/shard_map/reduce_scatter | solution.py:147
  197.6 1.5 multiply_convert_fusion.1
  (72 shorter events, 8.7 us)
Async XLA Ops:
  7.2 29.4 %copy-start.2 = (f32[2,128]{1,0:T(2,128)S(1)}, f32[2,128]{1,0:T(2,128)}, u32[]{:S(2)}) copy-start(f32[2,128]{1,0:T(2,128)} %param.15) | copy-start | bytes 3076
  7.2 46.8 %copy-start = (bf16[256,128]{1,0:T(8,128)(2,1)S(1)}, bf16[256,128]{1,0:T(8,128)(2,1)}, u32[]{:S(2)}) copy-start(bf16[256,128]{1,0:T(8,128)(2,1)} %param.11) | copy-start | bytes 196612
  7.2 51.9 %copy-start.1 = (bf16[256,128]{1,0:T(8,128)(2,1)S(1)}, bf16[256,128]{1,0:T(8,128)(2,1)}, u32[]{:S(2)}) copy-start(bf16[256,128]{1,0:T(8,128)(2,1)} %param.12) | copy-start | bytes 196612
  7.2 56.8 %all-gather.3.cloned.1.call-start = ((), (), s32[]{:S(2)}) async-start(), calls=%async_computation.3 | async-start | bytes 1114112 | tf_op jit(solution)/shard_map/all_gather | solution.py:133
  7.9 82.9 %all-gather.5.cloned.1.call-start = ((), (), s32[]{:S(2)}) async-start(), calls=%async_computation.4 | async-start | bytes 1114112 | tf_op jit(solution)/shard_map/all_gather | solution.py:134
  8.7 114.4 %reduce-scatter.8.cloned.1.call-start = ((), (), s32[]{:S(2)}) async-start(), calls=%async_computation.7 | async-start | bytes 393216 | tf_op jit(solution)/shard_map/reduce_scatter | solution.py:155
  107.8 24.6 %reduce-scatter.6.cloned.1.call-start = ((), (), s32[]{:S(2)}) async-start(), calls=%async_computation.6 | async-start | bytes 393216 | tf_op jit(solution)/shard_map/reduce_scatter | solution.py:154
  108.7 88.9 %reduce-scatter.4.cloned.1.call-start = ((), (), s32[]{:S(2)}) async-start(), calls=%async_computation.5 | async-start | bytes 2228224 | tf_op jit(solution)/shard_map/reduce_scatter | solution.py:147
Sparse Core Ops, SparseCore 0:
  10.2 41.5 all-gather.2
  53.9 36.8 all-gather.4
  107.9 10.6 reduce-scatter.7
  120.8 11.6 reduce-scatter.5
  136.0 61.5 reduce-scatter.3
where the time goes:
time: 206 us
  waiting for transfers between devices  99.6 us (48%)
  blocking collectives  53.7 us (26%)
  local copies, waits for them, and re-layouts  18.5 us (9%)
  between operations  13.9 us (7%)
  matrix products  12.7 us (6%)
  other arithmetic  6.47 us (3%)
    reduce_scatter x1, waiting for transfers between devices, per_device(): lax.psum_scatter(query_term(jnp.int32(0), queries.shape[0] * lax.axis_siz...  63.6 us
    all_gather x1, waiting for transfers between devices, per_device(): lax.all_gather(d_out, 'col', axis=0, tiled=True)  26.8 us
    all_gather x1, blocking collectives, per_device(): lax.all_gather(delta, 'col', axis=1, tiled=True)  26.3 us
    all_gather x1, blocking collectives, per_device(): lax.all_gather(lse, 'col', axis=1, tiled=True)  17.5 us
    squeeze x12, local copies, waits for them, and re-layouts, query_pass(): lax.scan(advance, (empty_sums, empty_sums), block_inputs)  12.1 us
    reduce_scatter x1, waiting for transfers between devices, per_device(): lax.psum_scatter(key_sum, 'row', scatter_dimension=1, tiled=True)  7.77 us
    dot_general x16, matrix products, contract_rows(): lax.dot_general(left, right, (((0,), (0,)), ((), ())), preferred_element_...  5.34 us
    all_gather x1, blocking collectives, per_device(): lax.all_gather(keys, 'row', axis=1, tiled=True)  5.02 us
  transfers between devices with their start and end apart: 5, of which 3 were waited for; matrix products, arithmetic and copies ran while one was open for 9% of the time, Pallas kernels for 0%

commit v1 on v0

--- a/solution.py
+++ b/solution.py
@@ -1,6 +1,10 @@
+import functools
+
 import jax
 import jax.numpy as jnp
 from jax import lax
+from jax.experimental import pallas as pl
+from jax.experimental.pallas import tpu as pltpu
 from jax.sharding import PartitionSpec as P
 
 
@@ -159,6 +163,288 @@
     d_values = value_grad.astype(jnp.bfloat16)
     return (d_queries, d_keys, d_values)
 
+LOG2E = 1.4426950408889634
+
+
+def flip(index, bits):
+    if bits == 1:
+        return index + 1 - 2 * lax.rem(index, 2)
+    if bits == 2:
+        return lax.rem(index + 2, 4)
+    if bits == 3:
+        return 3 - index
+    return index
+
+
+def fused_kernel(
+    head_total,
+    q_ref,
+    k_ref,
+    v_ref,
+    o_ref,
+    g_ref,
+    lse_ref,
+    dq_ref,
+    dk_ref,
+    dv_ref,
+    qd_out,
+    qd_in,
+    st_out,
+    st_in,
+    kv_in,
+    kt_in,
+    dk_acc,
+    dv_acc,
+    dq_out,
+    dq_in,
+    dkv_out,
+    dkv_in,
+    qd_ssem,
+    qd_rsem,
+    st_ssem,
+    st_rsem,
+    kv_ssem,
+    kv_rsem,
+    dq_ssem,
+    dq_rsem,
+    dkv_ssem,
+    dkv_rsem,
+):
+    row = lax.axis_index("row")
+    col = lax.axis_index("col")
+    zone = col // 4
+    lane = lax.rem(col, 4)
+    other = 1 - row
+    dim = k_ref.shape[1]
+    scaling = dim ** (-0.5)
+    MESH = pl.DeviceIdType.MESH
+
+    def at(r, z, m):
+        return (r, z * 4 + m)
+
+    mates = [at(row, zone, flip(lane, j)) for j in (1, 2, 3)]
+    owners = [at(other, zone, lane)]
+    for s in (1, 2, 3):
+        owners += [at(r, flip(zone, s), lane) for r in range(head_total)]
+    barrier = pltpu.get_barrier_semaphore()
+    for peer in mates + owners:
+        pl.semaphore_signal(barrier, inc=1, device_id=peer, device_id_type=MESH)
+
+    for h in range(head_total):
+        cols = slice(h * dim, (h + 1) * dim)
+        grad_part = g_ref[:, cols]
+        qd_out[h, 0] = q_ref[:, cols]
+        qd_out[h, 1] = grad_part
+        product = grad_part.astype(jnp.float32) * o_ref[:, cols].astype(jnp.float32)
+        delta = lax.dot_general(
+            jnp.ones((8, dim), jnp.float32),
+            product,
+            (((1,), (1,)), ((), ())),
+            precision=lax.Precision.HIGHEST,
+            preferred_element_type=jnp.float32,
+        )
+        lse_rows = jnp.broadcast_to(lse_ref[h : h + 1, :] * LOG2E, delta.shape)
+        upper = lax.broadcasted_iota(jnp.int32, delta.shape, 0) < 4
+        st_out[h] = jnp.where(upper, lse_rows, delta)
+    kv_in[lane, 0] = k_ref[...]
+    kv_in[lane, 1] = v_ref[...]
+    qd_in[zone, 0, row] = qd_out[row, 0]
+    qd_in[zone, 1, row] = qd_out[row, 1]
+    st_in[zone, row] = st_out[row]
+
+    pl.semaphore_wait(barrier, len(mates) + len(owners))
+
+    def kv_copy(j, slot):
+        return pltpu.make_async_remote_copy(
+            src_ref=kv_in.at[lane],
+            dst_ref=kv_in.at[slot],
+            send_sem=kv_ssem.at[j],
+            recv_sem=kv_rsem.at[slot],
+            device_id=at(row, zone, flip(lane, j)),
+            device_id_type=MESH,
+        )
+
+    def qd_copies(s, r, slot_zone, slot_row):
+        peer = at(r, flip(zone, s), lane)
+        return (
+            pltpu.make_async_remote_copy(
+                src_ref=st_out.at[r],
+                dst_ref=st_in.at[slot_zone, slot_row],
+                send_sem=st_ssem.at[s, r],
+                recv_sem=st_rsem.at[slot_zone, slot_row],
+                device_id=peer,
+                device_id_type=MESH,
+            ),
+            pltpu.make_async_remote_copy(
+                src_ref=qd_out.at[r],
+                dst_ref=qd_in.at[slot_zone, :, slot_row],
+                send_sem=qd_ssem.at[s, r],
+                recv_sem=qd_rsem.at[slot_zone, slot_row],
+                device_id=peer,
+                device_id_type=MESH,
+            ),
+        )
+
+    def rows_of(s):
+        return [other] if s == 0 else list(range(head_total))
+
+    sends = []
+
+    def launch(copy):
+        copy.start()
+        sends.append(copy)
+
+    for j in (2, 3, 1):
+        launch(kv_copy(j, lane))
+    for s in (0, 2, 3, 1):
+        for r in rows_of(s):
+            for copy in qd_copies(s, r, zone, row):
+                launch(copy)
+
+    def dq_copy(s, r, slot_row, slot_zone):
+        there = flip(zone, s)
+        return pltpu.make_async_remote_copy(
+            src_ref=dq_out.at[there, r],
+            dst_ref=dq_in.at[slot_row, slot_zone],
+            send_sem=dq_ssem.at[s, r],
+            recv_sem=dq_rsem.at[slot_row, slot_zone],
+            device_id=at(r, there, lane),
+            device_id_type=MESH,
+        )
+
+    def dkv_copy(j, slot):
+        there = flip(lane, j)
+        return pltpu.make_async_remote_copy(
+            src_ref=dkv_out.at[there],
+            dst_ref=dkv_in.at[slot],
+            send_sem=dkv_ssem.at[j],
+            recv_sem=dkv_rsem.at[slot],
+            device_id=at(row, zone, there),
+            device_id_type=MESH,
+        )
+
+    steps = (0, 1, 2, 3)
+    for s in steps:
+        there = flip(zone, s)
+        for r in rows_of(s):
+            for copy in qd_copies(s, r, there, r):
+                copy.wait_recv()
+        rows2 = head_total * q_ref.shape[0]
+        query = qd_in[there, 0].reshape(rows2, dim)
+        grad = qd_in[there, 1].reshape(rows2, dim)
+        lse_row = jnp.concatenate([st_in[there, r, 0:1, :] for r in range(head_total)], axis=1)
+        delta_row = jnp.concatenate([st_in[there, r, 4:5, :] for r in range(head_total)], axis=1)
+        query_sum = None
+        order = (0, 1, 2, 3) if s < 3 else (2, 3, 1, 0)
+        for j in order:
+            slot = flip(lane, j)
+            if s == 0:
+                if j > 0:
+                    kv_copy(j, slot).wait_recv()
+                kt_in[slot] = kv_in[slot, 0].T
+            key = kv_in[slot, 0]
+            value = kv_in[slot, 1]
+            dims = (((1,), (1,)), ((), ()))
+            scores = lax.dot_general(key, query, dims, preferred_element_type=jnp.float32)
+            grad_probs = lax.dot_general(value, grad, dims, preferred_element_type=jnp.float32)
+            probs = jnp.exp2(scores * (scaling * LOG2E) - lse_row)
+            probs_low = probs.astype(jnp.bfloat16)
+            grad_scores = (probs * (grad_probs - delta_row)).astype(jnp.bfloat16)
+            value_term = jnp.dot(probs_low, grad, preferred_element_type=jnp.float32)
+            key_term = jnp.dot(grad_scores, query, preferred_element_type=jnp.float32)
+            query_term = jnp.dot(kt_in[slot], grad_scores, preferred_element_type=jnp.float32)
+            query_sum = query_term if query_sum is None else query_sum + query_term
+            if s > 0:
+                key_term = dk_acc[slot] + key_term
+                value_term = dv_acc[slot] + value_term
+            if s == 3 and j > 0:
+                dkv_out[slot, 0] = key_term.astype(jnp.bfloat16)
+                dkv_out[slot, 1] = value_term.astype(jnp.bfloat16)
+                launch(dkv_copy(j, lane))
+            else:
+                dk_acc[slot] = key_term
+                dv_acc[slot] = value_term
+        query_low = query_sum.astype(jnp.bfloat16)
+        block = q_ref.shape[0]
+        for r in range(head_total):
+            dq_out[there, r] = query_low[:, r * block : (r + 1) * block]
+        if s == 0:
+            dq_in[row, zone] = dq_out[zone, row]
+        for r in rows_of(s):
+            launch(dq_copy(s, r, row, zone))
+
+    for s in steps:
+        for r in rows_of(s):
+            dq_copy(s, r, r, flip(zone, s)).wait_recv()
+    for h in range(head_total):
+        total = dq_in[h, 0].astype(jnp.float32)
+        for z in range(1, 4):
+            total = total + dq_in[h, z].astype(jnp.float32)
+        dq_ref[:, h * dim : (h + 1) * dim] = (total * scaling).T.astype(jnp.bfloat16)
+
+    key_sum = dk_acc[lane]
+    value_sum = dv_acc[lane]
+    for j in (1, 2, 3):
+        slot = flip(lane, j)
+        dkv_copy(j, slot).wait_recv()
+        key_sum = key_sum + dkv_in[slot, 0].astype(jnp.float32)
+        value_sum = value_sum + dkv_in[slot, 1].astype(jnp.float32)
+    dk_ref[...] = (key_sum * scaling).astype(jnp.bfloat16)
+    dv_ref[...] = value_sum.astype(jnp.bfloat16)
+    for copy in sends:
+        copy.wait_send()
+
+
+def fused_device(queries, keys, values, outputs, d_out, lse):
+    head_total = lse.shape[0]
+    block = queries.shape[0]
+    key_rows, dim = keys.shape
+    zones, lanes = 4, 4
+    bf16, f32 = jnp.bfloat16, jnp.float32
+    dma = pltpu.SemaphoreType.DMA
+    vmem = pl.BlockSpec(memory_space=pltpu.VMEM)
+    pairs = head_total * block * zones * key_rows * lanes
+    return pl.pallas_call(
+        functools.partial(fused_kernel, head_total),
+        out_shape=(
+            jax.ShapeDtypeStruct(queries.shape, bf16),
+            jax.ShapeDtypeStruct(keys.shape, bf16),
+            jax.ShapeDtypeStruct(values.shape, bf16),
+        ),
+        in_specs=[vmem] * 6,
+        out_specs=(vmem, vmem, vmem),
+        scratch_shapes=[
+            pltpu.VMEM((head_total, 2, block, dim), bf16),
+            pltpu.VMEM((zones, 2, head_total, block, dim), bf16),
+            pltpu.VMEM((head_total, 8, block), f32),
+            pltpu.VMEM((zones, head_total, 8, block), f32),
+            pltpu.VMEM((lanes, 2, key_rows, dim), bf16),
+            pltpu.VMEM((lanes, dim, key_rows), bf16),
+            pltpu.VMEM((lanes, key_rows, dim), f32),
+            pltpu.VMEM((lanes, key_rows, dim), f32),
+            pltpu.VMEM((zones, head_total, dim, block), bf16),
+            pltpu.VMEM((head_total, zones, dim, block), bf16),
+            pltpu.VMEM((lanes, 2, key_rows, dim), bf16),
+            pltpu.VMEM((lanes, 2, key_rows, dim), bf16),
+            dma((zones, head_total)),
+            dma((zones, head_total)),
+            dma((zones, head_total)),
+            dma((zones, head_total)),
+            dma((lanes,)),
+            dma((lanes,)),
+            dma((zones, head_total)),
+            dma((head_total, zones)),
+            dma((lanes,)),
+            dma((lanes,)),
+        ],
+        compiler_params=pltpu.CompilerParams(
+            collective_id=0, has_side_effects=True, vmem_limit_bytes=32 * 1024 * 1024
+        ),
+        cost_estimate=pl.CostEstimate(
+            flops=10 * pairs * dim, bytes_accessed=9 * block * 2 * dim * 2, transcendentals=pairs
+        ),
+    )(queries, keys, values, outputs, d_out, lse)
+
 
 def solution(mesh):
     placed = (
@@ -169,8 +455,16 @@
         P(("row", "col"), None),
         P(None, ("row", "col")),
     )
+    fused = mesh.shape["row"] == 2 and mesh.shape["col"] == 16
+
+    def local(queries, keys, values, outputs, d_out, lse):
+        head_dim = queries.shape[1] // lse.shape[0]
+        fits = lse.shape[0] == mesh.shape["row"] and head_dim == 128 and queries.shape[0] == 128
+        chosen = fused_device if fused and fits else per_device
+        return chosen(queries, keys, values, outputs, d_out, lse)
+
     return jax.shard_map(
-        per_device,
+        local,
         mesh=mesh,
         in_specs=placed,
         out_specs=(P(("row", "col"), None), P("col", "row"), P("col", "row")),

time: 206 us -> 34.6 us (0.17)
  the two profiles are of different devices: /device:TPU:0 before, /device:TPU:8 now
where the time goes in v1:
time: 34.6 us; the launch traced here: 34.2 us
  Pallas kernels  26.8 us (77%)
  local copies, waits for them, and re-layouts  6.76 us (20%)
  between operations  0.65 us (2%)
    pallas_call x1, Pallas kernels, fused_device(): pl.pallas_call(functools.partial(fused_kernel, head_total), out_shape=(ja...  26.8 us
    unnamed x15, local copies, waits for them, and re-layouts  6.76 us

profile of v1, /device:TPU:8, one launch (start us, length us, event | category | flops | bytes accessed | tf_op | source)
XLA Modules:
  0.0 34.2 jit_solution(9542925236196155395)
XLA Ops:
  0.6 0.0 copy-start
  0.6 0.8 %copy-done = bf16[128,256]{1,0:T(8,128)(2,1)S(1)} copy-done((bf16[128,256]{1,0:T(8,128)(2,1)S(1)}, bf16[128,256]{1,0:T(8,128)(2,1)}, u32[]{:S(2)}) %copy-start) | copy-done | bytes 65560
  1.5 0.0 copy-start.1
  1.5 0.8 %copy-done.1 = bf16[256,128]{1,0:T(8,128)(2,1)S(1)} copy-done((bf16[256,128]{1,0:T(8,128)(2,1)S(1)}, bf16[256,128]{1,0:T(8,128)(2,1)}, u32[]{:S(2)}) %copy-start.1) | copy-done | bytes 65560
  2.3 0.0 copy-start.2
  2.3 0.8 %copy-done.2 = bf16[256,128]{1,0:T(8,128)(2,1)S(1)} copy-done((bf16[256,128]{1,0:T(8,128)(2,1)S(1)}, bf16[256,128]{1,0:T(8,128)(2,1)}, u32[]{:S(2)}) %copy-start.2) | copy-done | bytes 65560
  3.2 0.0 copy-start.3
  3.2 0.8 %copy-done.3 = bf16[128,256]{1,0:T(8,128)(2,1)S(1)} copy-done((bf16[128,256]{1,0:T(8,128)(2,1)S(1)}, bf16[128,256]{1,0:T(8,128)(2,1)}, u32[]{:S(2)}) %copy-start.3) | copy-done | bytes 65560
  4.0 0.0 copy-start.4
  4.0 0.8 %copy-done.4 = bf16[128,256]{1,0:T(8,128)(2,1)S(1)} copy-done((bf16[128,256]{1,0:T(8,128)(2,1)S(1)}, bf16[128,256]{1,0:T(8,128)(2,1)}, u32[]{:S(2)}) %copy-start.4) | copy-done | bytes 65560
  4.8 0.0 copy-start.5
  4.8 0.7 %copy-done.5 = f32[2,128]{1,0:T(2,128)S(1)} copy-done((f32[2,128]{1,0:T(2,128)S(1)}, f32[2,128]{1,0:T(2,128)}, u32[]{:S(2)}) %copy-start.5) | copy-done | bytes 1048
  5.5 26.8 %shard_map.85 = (bf16[128,256]{1,0:T(8,128)(2,1)S(1)}, bf16[256,128]{1,0:T(8,128)(2,1)S(1)}, bf16[256,128]{1,0:T(8,128)(2,1)S(1)}) custom-call(bf16[128,256]{1,0:T(8,128)(2,1)S(1)} %copy-done, bf16[256,128]{1,0:T(8,128)(2,1)S(1)} %copy-done.1, bf16[256,128]{1,0:T(8,128)(2,1)S(1)} %copy-done.2, bf16[128,256]{1,0:T(8,128)(2,1)S(1)} %copy-done.3, ...), custom_call_target="tpu_custom_call" | custom-call | flops 1342177280 | bytes 589824 | tf_op jit(solution)/shard_map/pallas_call | solution.py:407
  32.3 0.6 %copy.12 = bf16[128,256]{1,0:T(8,128)(2,1)} copy(bf16[128,256]{1,0:T(8,128)(2,1)S(1)} %get-tuple-element.6) | data formatting | bytes 131072
  33.0 0.6 %copy.13 = bf16[256,128]{1,0:T(8,128)(2,1)} copy(bf16[256,128]{1,0:T(8,128)(2,1)S(1)} %get-tuple-element.7) | data formatting | bytes 131072
  33.6 0.6 %copy.14 = bf16[256,128]{1,0:T(8,128)(2,1)} copy(bf16[256,128]{1,0:T(8,128)(2,1)S(1)} %get-tuple-element.8) | data formatting | bytes 131072
Async XLA Ops:
  0.6 0.8 %copy-start = (bf16[128,256]{1,0:T(8,128)(2,1)S(1)}, bf16[128,256]{1,0:T(8,128)(2,1)}, u32[]{:S(2)}) copy-start(bf16[128,256]{1,0:T(8,128)(2,1)} %q_ref.1) | copy-start | bytes 196612
  1.5 0.8 %copy-start.1 = (bf16[256,128]{1,0:T(8,128)(2,1)S(1)}, bf16[256,128]{1,0:T(8,128)(2,1)}, u32[]{:S(2)}) copy-start(bf16[256,128]{1,0:T(8,128)(2,1)} %k_ref.1) | copy-start | bytes 196612
  2.3 0.8 %copy-start.2 = (bf16[256,128]{1,0:T(8,128)(2,1)S(1)}, bf16[256,128]{1,0:T(8,128)(2,1)}, u32[]{:S(2)}) copy-start(bf16[256,128]{1,0:T(8,128)(2,1)} %v_ref.1) | copy-start | bytes 196612
  3.2 0.8 %copy-start.3 = (bf16[128,256]{1,0:T(8,128)(2,1)S(1)}, bf16[128,256]{1,0:T(8,128)(2,1)}, u32[]{:S(2)}) copy-start(bf16[128,256]{1,0:T(8,128)(2,1)} %o_ref.1) | copy-start | bytes 196612
  4.0 0.8 %copy-start.4 = (bf16[128,256]{1,0:T(8,128)(2,1)S(1)}, bf16[128,256]{1,0:T(8,128)(2,1)}, u32[]{:S(2)}) copy-start(bf16[128,256]{1,0:T(8,128)(2,1)} %g_ref.1) | copy-start | bytes 196612
  4.8 0.7 %copy-start.5 = (f32[2,128]{1,0:T(2,128)S(1)}, f32[2,128]{1,0:T(2,128)}, u32[]{:S(2)}) copy-start(f32[2,128]{1,0:T(2,128)} %lse_ref.1) | copy-start | bytes 3076

commit v2 on v1

--- a/solution.py
+++ b/solution.py
@@ -209,18 +209,37 @@
     dq_rsem,
     dkv_ssem,
     dkv_rsem,
+    o_in,
+    lse_in,
+    in_sem,
 ):
     row = lax.axis_index("row")
     col = lax.axis_index("col")
-    zone = col // 4
-    lane = lax.rem(col, 4)
+    zone = (col // 8) * 2 + lax.rem(col, 2)
+    lane = lax.rem(col, 8) // 2
     other = 1 - row
     dim = k_ref.shape[1]
     scaling = dim ** (-0.5)
     MESH = pl.DeviceIdType.MESH
 
     def at(r, z, m):
-        return (r, z * 4 + m)
+        return (r, (z // 2) * 8 + m * 2 + lax.rem(z, 2))
+
+    loads = []
+    for h in range(head_total):
+        cols = pl.ds(h * dim, dim)
+        loads.append(pltpu.make_async_copy(q_ref.at[:, cols], qd_out.at[h, 0], in_sem.at[2 * h]))
+        loads.append(pltpu.make_async_copy(g_ref.at[:, cols], qd_out.at[h, 1], in_sem.at[2 * h + 1]))
+    key_loads = [
+        pltpu.make_async_copy(k_ref, kv_in.at[lane, 0], in_sem.at[4]),
+        pltpu.make_async_copy(v_ref, kv_in.at[lane, 1], in_sem.at[5]),
+    ]
+    row_loads = [
+        pltpu.make_async_copy(o_ref, o_in, in_sem.at[6]),
+        pltpu.make_async_copy(lse_ref, lse_in, in_sem.at[7]),
+    ]
+    for load in loads + key_loads + row_loads:
+        load.start()
 
     mates = [at(row, zone, flip(lane, j)) for j in (1, 2, 3)]
     owners = [at(other, zone, lane)]
@@ -229,30 +248,6 @@
     barrier = pltpu.get_barrier_semaphore()
     for peer in mates + owners:
         pl.semaphore_signal(barrier, inc=1, device_id=peer, device_id_type=MESH)
-
-    for h in range(head_total):
-        cols = slice(h * dim, (h + 1) * dim)
-        grad_part = g_ref[:, cols]
-        qd_out[h, 0] = q_ref[:, cols]
-        qd_out[h, 1] = grad_part
-        product = grad_part.astype(jnp.float32) * o_ref[:, cols].astype(jnp.float32)
-        delta = lax.dot_general(
-            jnp.ones((8, dim), jnp.float32),
-            product,
-            (((1,), (1,)), ((), ())),
-            precision=lax.Precision.HIGHEST,
-            preferred_element_type=jnp.float32,
-        )
-        lse_rows = jnp.broadcast_to(lse_ref[h : h + 1, :] * LOG2E, delta.shape)
-        upper = lax.broadcasted_iota(jnp.int32, delta.shape, 0) < 4
-        st_out[h] = jnp.where(upper, lse_rows, delta)
-    kv_in[lane, 0] = k_ref[...]
-    kv_in[lane, 1] = v_ref[...]
-    qd_in[zone, 0, row] = qd_out[row, 0]
-    qd_in[zone, 1, row] = qd_out[row, 1]
-    st_in[zone, row] = st_out[row]
-
-    pl.semaphore_wait(barrier, len(mates) + len(owners))
 
     def kv_copy(j, slot):
         return pltpu.make_async_remote_copy(
@@ -264,25 +259,34 @@
             device_id_type=MESH,
         )
 
-    def qd_copies(s, r, slot_zone, slot_row):
-        peer = at(r, flip(zone, s), lane)
-        return (
-            pltpu.make_async_remote_copy(
-                src_ref=st_out.at[r],
-                dst_ref=st_in.at[slot_zone, slot_row],
-                send_sem=st_ssem.at[s, r],
-                recv_sem=st_rsem.at[slot_zone, slot_row],
-                device_id=peer,
-                device_id_type=MESH,
-            ),
-            pltpu.make_async_remote_copy(
-                src_ref=qd_out.at[r],
-                dst_ref=qd_in.at[slot_zone, :, slot_row],
-                send_sem=qd_ssem.at[s, r],
-                recv_sem=qd_rsem.at[slot_zone, slot_row],
-                device_id=peer,
-                device_id_type=MESH,
-            ),
+    def st_copy(s, r, slot_zone, slot_row):
+        return pltpu.make_async_remote_copy(
+            src_ref=st_out.at[r],
+            dst_ref=st_in.at[slot_zone, slot_row],
+            send_sem=st_ssem.at[s, r],
+            recv_sem=st_rsem.at[slot_zone, slot_row],
+            device_id=at(r, flip(zone, s), lane),
+            device_id_type=MESH,
+        )
+
+    def qd_copy(s, r, slot_zone, slot_row):
+        return pltpu.make_async_remote_copy(
+            src_ref=qd_out.at[r],
+            dst_ref=qd_in.at[slot_zone, :, slot_row],
+            send_sem=qd_ssem.at[s, r],
+            recv_sem=qd_rsem.at[slot_zone, slot_row],
+            device_id=at(r, flip(zone, s), lane),
+            device_id_type=MESH,
+        )
+
+    def pass_copy(s, r, slot_zone):
+        return pltpu.make_async_remote_copy(
+            src_ref=qd_in.at[slot_zone, :, r],
+            dst_ref=qd_in.at[slot_zone, :, r],
+            send_sem=qd_ssem.at[s + 1, r],
+            recv_sem=qd_rsem.at[slot_zone, r],
+            device_id=at(row, flip(zone, 1), lane),
+            device_id_type=MESH,
         )
 
     def rows_of(s):
@@ -294,12 +298,39 @@
         copy.start()
         sends.append(copy)
 
-    for j in (2, 3, 1):
+    for load in loads:
+        load.wait()
+    pl.semaphore_wait(barrier, len(mates) + len(owners))
+    for s in (2, 0):
+        for r in rows_of(s):
+            launch(qd_copy(s, r, zone, row))
+    for load in key_loads:
+        load.wait()
+    for j in (1, 2, 3):
         launch(kv_copy(j, lane))
-    for s in (0, 2, 3, 1):
+    qd_in[zone, 0, row] = qd_out[row, 0]
+    qd_in[zone, 1, row] = qd_out[row, 1]
+    launch(pass_copy(0, row, zone))
+
+    for load in row_loads:
+        load.wait()
+    for h in range(head_total):
+        cols = slice(h * dim, (h + 1) * dim)
+        product = qd_out[h, 1].astype(jnp.float32) * o_in[:, cols].astype(jnp.float32)
+        delta = lax.dot_general(
+            jnp.ones((8, dim), jnp.float32),
+            product,
+            (((1,), (1,)), ((), ())),
+            precision=lax.Precision.HIGHEST,
+            preferred_element_type=jnp.float32,
+        )
+        lse_rows = jnp.broadcast_to(lse_in[h : h + 1, :] * LOG2E, delta.shape)
+        upper = lax.broadcasted_iota(jnp.int32, delta.shape, 0) < 4
+        st_out[h] = jnp.where(upper, lse_rows, delta)
+    st_in[zone, row] = st_out[row]
+    for s in (2, 0, 3, 1):
         for r in rows_of(s):
-            for copy in qd_copies(s, r, zone, row):
-                launch(copy)
+            launch(st_copy(s, r, zone, row))
 
     def dq_copy(s, r, slot_row, slot_zone):
         there = flip(zone, s)
@@ -327,8 +358,11 @@
     for s in steps:
         there = flip(zone, s)
         for r in rows_of(s):
-            for copy in qd_copies(s, r, there, r):
-                copy.wait_recv()
+            qd_copy(s, r, there, r).wait_recv()
+            if s in (0, 2):
+                launch(pass_copy(s, r, there))
+        for r in rows_of(s):
+            st_copy(s, r, there, r).wait_recv()
         rows2 = head_total * q_ref.shape[0]
         query = qd_in[there, 0].reshape(rows2, dim)
         grad = qd_in[there, 1].reshape(rows2, dim)
@@ -411,7 +445,7 @@
             jax.ShapeDtypeStruct(keys.shape, bf16),
             jax.ShapeDtypeStruct(values.shape, bf16),
         ),
-        in_specs=[vmem] * 6,
+        in_specs=[pl.BlockSpec(memory_space=pltpu.HBM)] * 6,
         out_specs=(vmem, vmem, vmem),
         scratch_shapes=[
             pltpu.VMEM((head_total, 2, block, dim), bf16),
@@ -436,9 +470,12 @@
             dma((head_total, zones)),
             dma((lanes,)),
             dma((lanes,)),
+            pltpu.VMEM(outputs.shape, bf16),
+            pltpu.VMEM(lse.shape, f32),
+            dma((8,)),
         ],
         compiler_params=pltpu.CompilerParams(
-            collective_id=0, has_side_effects=True, vmem_limit_bytes=32 * 1024 * 1024
+            collective_id=0, has_side_effects=True, vmem_limit_bytes=63 * 1024 * 1024
         ),
         cost_estimate=pl.CostEstimate(
             flops=10 * pairs * dim, bytes_accessed=9 * block * 2 * dim * 2, transcendentals=pairs

time: 34.6 us -> 35.1 us (1.014)
  the two profiles are of different devices: /device:TPU:8 before, /device:TPU:0 now
where the time goes in v2:
time: 35.1 us; the launch traced here: 34.8 us
  Pallas kernels  31.2 us (89%)
  local copies, waits for them, and re-layouts  3 us (9%)
  between operations  0.65 us (2%)
    pallas_call x1, Pallas kernels, fused_device(): pl.pallas_call(functools.partial(fused_kernel, head_total), out_shape=(ja...  31.2 us
    unnamed x7, local copies, waits for them, and re-layouts  3 us

profile of v2, /device:TPU:0, one launch (start us, length us, event | category | flops | bytes accessed | tf_op | source)
XLA Modules:
  0.0 34.8 jit_solution(16090281847946439586)
XLA Ops:
  0.6 31.2 %shard_map.85 = (bf16[128,256]{1,0:T(8,128)(2,1)}, bf16[256,128]{1,0:T(8,128)(2,1)}, bf16[256,128]{1,0:T(8,128)(2,1)}) custom-call(bf16[128,256]{1,0:T(8,128)(2,1)} %q_ref.1, bf16[256,128]{1,0:T(8,128)(2,1)} %k_ref.1, bf16[256,128]{1,0:T(8,128)(2,1)} %v_ref.1, bf16[128,256]{1,0:T(8,128)(2,1)} %o_ref.1, bf16[128,256]{1,0:T(8,128)(2,1)} %g_ref.1, f32[2,128]{1,0:T(2,128)} %lse_ref.1), custom_call_target="tpu_custom_call" | custom-call | flops 1342177280 | bytes 589824 | tf_op jit(solution)/shard_map/pallas_call | solution.py:441
  31.8 0.0 copy-start.1
  31.8 1.5 %copy.12 = bf16[128,256]{1,0:T(8,128)(2,1)} copy(bf16[128,256]{1,0:T(8,128)(2,1)} %get-tuple-element.6) | data formatting | bytes 131072
  33.3 0.0 copy-done.1
  33.3 0.0 copy-start
  33.3 0.6 %copy.13 = bf16[256,128]{1,0:T(8,128)(2,1)} copy(bf16[256,128]{1,0:T(8,128)(2,1)S(1)} %copy-done.1) | data formatting | bytes 131072
  33.9 0.2 copy-done
  34.2 0.6 %copy.14 = bf16[256,128]{1,0:T(8,128)(2,1)} copy(bf16[256,128]{1,0:T(8,128)(2,1)S(1)} %copy-done) | data formatting | bytes 131072
Async XLA Ops:
  31.8 1.5 %copy-start.1 = (bf16[256,128]{1,0:T(8,128)(2,1)S(1)}, bf16[256,128]{1,0:T(8,128)(2,1)}, u32[]{:S(2)}) copy-start(bf16[256,128]{1,0:T(8,128)(2,1)} %get-tuple-element.7) | copy-start | bytes 196612
  33.3 0.9 %copy-start = (bf16[256,128]{1,0:T(8,128)(2,1)S(1)}, bf16[256,128]{1,0:T(8,128)(2,1)}, u32[]{:S(2)}) copy-start(bf16[256,128]{1,0:T(8,128)(2,1)} %get-tuple-element.8) | copy-start | bytes 196612

commit v3 on v2

--- a/solution.py
+++ b/solution.py
@@ -212,18 +212,20 @@
     o_in,
     lse_in,
     in_sem,
+    relay_ssem,
 ):
     row = lax.axis_index("row")
     col = lax.axis_index("col")
-    zone = (col // 8) * 2 + lax.rem(col, 2)
-    lane = lax.rem(col, 8) // 2
+    zone = col // 4
+    lane = lax.rem(col, 4)
+    inner = lax.rem(zone + 1, 4) // 2 == 1
     other = 1 - row
     dim = k_ref.shape[1]
     scaling = dim ** (-0.5)
     MESH = pl.DeviceIdType.MESH
 
     def at(r, z, m):
-        return (r, (z // 2) * 8 + m * 2 + lax.rem(z, 2))
+        return (r, z * 4 + m)
 
     loads = []
     for h in range(head_total):
@@ -279,11 +281,12 @@
             device_id_type=MESH,
         )
 
-    def pass_copy(s, r, slot_zone):
+    def relay_copy(r):
+        slot_zone = flip(zone, 2)
         return pltpu.make_async_remote_copy(
             src_ref=qd_in.at[slot_zone, :, r],
             dst_ref=qd_in.at[slot_zone, :, r],
-            send_sem=qd_ssem.at[s + 1, r],
+            send_sem=relay_ssem.at[r],
             recv_sem=qd_rsem.at[slot_zone, r],
             device_id=at(row, flip(zone, 1), lane),
             device_id_type=MESH,
@@ -301,16 +304,23 @@
     for load in loads:
         load.wait()
     pl.semaphore_wait(barrier, len(mates) + len(owners))
-    for s in (2, 0):
+    for r in rows_of(2):
+        launch(qd_copy(2, r, zone, row))
+
+    @pl.when(inner)
+    def _():
+        for r in rows_of(3):
+            qd_copy(3, r, zone, row).start()
+
+    for load in key_loads:
+        load.wait()
+    for j in (2, 3, 1):
+        launch(kv_copy(j, lane))
+    for s in (0, 1):
         for r in rows_of(s):
             launch(qd_copy(s, r, zone, row))
-    for load in key_loads:
-        load.wait()
-    for j in (1, 2, 3):
-        launch(kv_copy(j, lane))
     qd_in[zone, 0, row] = qd_out[row, 0]
     qd_in[zone, 1, row] = qd_out[row, 1]
-    launch(pass_copy(0, row, zone))
 
     for load in row_loads:
         load.wait()
@@ -354,13 +364,18 @@
             device_id_type=MESH,
         )
 
-    steps = (0, 1, 2, 3)
+    steps = (0, 2, 1, 3)
     for s in steps:
         there = flip(zone, s)
         for r in rows_of(s):
             qd_copy(s, r, there, r).wait_recv()
-            if s in (0, 2):
-                launch(pass_copy(s, r, there))
+        if s == 2:
+
+            @pl.when(inner)
+            def _():
+                for r in rows_of(2):
+                    relay_copy(r).start()
+
         for r in rows_of(s):
             st_copy(s, r, there, r).wait_recv()
         rows2 = head_total * q_ref.shape[0]
@@ -428,6 +443,21 @@
     for copy in sends:
         copy.wait_send()
 
+    @pl.when(inner)
+    def _():
+        for r in rows_of(3):
+            qd_copy(3, r, zone, row).wait_send()
+            relay_copy(r).wait_send()
+
+
+def write_kernel(dq_ref, dk_ref, dv_ref, dq_out, dk_out, dv_out, sems):
+    pairs = ((dq_ref, dq_out), (dk_ref, dk_out), (dv_ref, dv_out))
+    copies = [pltpu.make_async_copy(src, dst, sems.at[i]) for i, (src, dst) in enumerate(pairs)]
+    for copy in copies:
+        copy.start()
+    for copy in copies:
+        copy.wait()
+
 
 def fused_device(queries, keys, values, outputs, d_out, lse):
     head_total = lse.shape[0]
@@ -438,14 +468,15 @@
     dma = pltpu.SemaphoreType.DMA
     vmem = pl.BlockSpec(memory_space=pltpu.VMEM)
     pairs = head_total * block * zones * key_rows * lanes
-    return pl.pallas_call(
+    hbm = pl.BlockSpec(memory_space=pltpu.HBM)
+    results = pl.pallas_call(
         functools.partial(fused_kernel, head_total),
         out_shape=(
             jax.ShapeDtypeStruct(queries.shape, bf16),
             jax.ShapeDtypeStruct(keys.shape, bf16),
             jax.ShapeDtypeStruct(values.shape, bf16),
         ),
-        in_specs=[pl.BlockSpec(memory_space=pltpu.HBM)] * 6,
+        in_specs=[hbm] * 6,
         out_specs=(vmem, vmem, vmem),
         scratch_shapes=[
             pltpu.VMEM((head_total, 2, block, dim), bf16),
@@ -473,6 +504,7 @@
             pltpu.VMEM(outputs.shape, bf16),
             pltpu.VMEM(lse.shape, f32),
             dma((8,)),
+            dma((head_total,)),
         ],
         compiler_params=pltpu.CompilerParams(
             collective_id=0, has_side_effects=True, vmem_limit_bytes=63 * 1024 * 1024
@@ -481,6 +513,14 @@
             flops=10 * pairs * dim, bytes_accessed=9 * block * 2 * dim * 2, transcendentals=pairs
         ),
     )(queries, keys, values, outputs, d_out, lse)
+    return pl.pallas_call(
+        write_kernel,
+        out_shape=tuple(jax.ShapeDtypeStruct(x.shape, x.dtype) for x in results),
+        in_specs=[hbm] * 3,
+        out_specs=(hbm, hbm, hbm),
+        scratch_shapes=[dma((3,))],
+        compiler_params=pltpu.CompilerParams(vmem_limit_bytes=63 * 1024 * 1024),
+    )(*results)
 
 
 def solution(mesh):

time: 35.1 us -> 35.1 us (level)
  Pallas kernels: 31.2 us -> 34.2 us
  local copies, waits for them, and re-layouts: 3 us -> 0 us
    pallas_call x0 -> x1, Pallas kernels: none -> 7.09 us  [fused_device(): pl.pallas_call(write_kernel, out_shape=tuple((jax.ShapeDtypeStruct(x.shap...]
    pallas_call x1, Pallas kernels: 31.2 us -> 27.1 us  [fused_device(): pl.pallas_call(functools.partial(fused_kernel, head_total), out_shape=(ja...]
    unnamed x7 -> x0, local copies, waits for them, and re-layouts: 3 us -> none
where the time goes in v3:
time: 35.1 us; the launch traced here: 34.8 us
  Pallas kernels  34.2 us (97%)
  between operations  0.64 us (2%)
    pallas_call x1, Pallas kernels, fused_device(): pl.pallas_call(functools.partial(fused_kernel, head_total), out_shape=(ja...  27.1 us
    pallas_call x1, Pallas kernels, fused_device(): pl.pallas_call(write_kernel, out_shape=tuple((jax.ShapeDtypeStruct(x.shap...  7.09 us

profile of v3, /device:TPU:0, one launch (start us, length us, event | category | flops | bytes accessed | tf_op | source)
XLA Modules:
  0.0 34.8 jit_solution(6575616922506629600)
XLA Ops:
  0.6 27.1 %shard_map.85 = (bf16[128,256]{1,0:T(8,128)(2,1)}, bf16[256,128]{1,0:T(8,128)(2,1)}, bf16[256,128]{1,0:T(8,128)(2,1)}) custom-call(bf16[128,256]{1,0:T(8,128)(2,1)} %q_ref.1, bf16[256,128]{1,0:T(8,128)(2,1)} %k_ref.1, bf16[256,128]{1,0:T(8,128)(2,1)} %v_ref.1, bf16[128,256]{1,0:T(8,128)(2,1)} %o_ref.1, bf16[128,256]{1,0:T(8,128)(2,1)} %g_ref.1, f32[2,128]{1,0:T(2,128)} %lse_ref.1), custom_call_target="tpu_custom_call" | custom-call | flops 1342177280 | bytes 589824 | tf_op jit(solution)/shard_map/pallas_call | solution.py:472
  27.8 7.1 %shard_map.86 = (bf16[128,256]{1,0:T(8,128)(2,1)}, bf16[256,128]{1,0:T(8,128)(2,1)}, bf16[256,128]{1,0:T(8,128)(2,1)}) custom-call(bf16[128,256]{1,0:T(8,128)(2,1)} %get-tuple-element.6.dq_ref, bf16[256,128]{1,0:T(8,128)(2,1)} %get-tuple-element.7.dk_ref, bf16[256,128]{1,0:T(8,128)(2,1)} %get-tuple-element.8.dv_ref), custom_call_target="tpu_custom_call" | custom-call | tf_op jit(solution)/shard_map/pallas_call | solution.py:516

commit v4 on v3

--- a/solution.py
+++ b/solution.py
@@ -243,7 +243,7 @@
     for load in loads + key_loads + row_loads:
         load.start()
 
-    mates = [at(row, zone, flip(lane, j)) for j in (1, 2, 3)]
+    mates = [at(row, zone, flip(lane, j)) for j in (1, 2)]
     owners = [at(other, zone, lane)]
     for s in (1, 2, 3):
         owners += [at(r, flip(zone, s), lane) for r in range(head_total)]
@@ -261,6 +261,17 @@
             device_id_type=MESH,
         )
 
+    def kv_pass():
+        slot = flip(lane, 2)
+        return pltpu.make_async_remote_copy(
+            src_ref=kv_in.at[slot],
+            dst_ref=kv_in.at[slot],
+            send_sem=kv_ssem.at[3],
+            recv_sem=kv_rsem.at[slot],
+            device_id=at(row, zone, flip(lane, 1)),
+            device_id_type=MESH,
+        )
+
     def st_copy(s, r, slot_zone, slot_row):
         return pltpu.make_async_remote_copy(
             src_ref=st_out.at[r],
@@ -306,15 +317,9 @@
     pl.semaphore_wait(barrier, len(mates) + len(owners))
     for r in rows_of(2):
         launch(qd_copy(2, r, zone, row))
-
-    @pl.when(inner)
-    def _():
-        for r in rows_of(3):
-            qd_copy(3, r, zone, row).start()
-
     for load in key_loads:
         load.wait()
-    for j in (2, 3, 1):
+    for j in (2, 1):
         launch(kv_copy(j, lane))
     for s in (0, 1):
         for r in rows_of(s):
@@ -353,14 +358,13 @@
             device_id_type=MESH,
         )
 
-    def dkv_copy(j, slot):
-        there = flip(lane, j)
-        return pltpu.make_async_remote_copy(
-            src_ref=dkv_out.at[there],
-            dst_ref=dkv_in.at[slot],
+    def dkv_copy(j):
+        return pltpu.make_async_remote_copy(
+            src_ref=dkv_out.at[j],
+            dst_ref=dkv_in.at[j],
             send_sem=dkv_ssem.at[j],
-            recv_sem=dkv_rsem.at[slot],
-            device_id=at(row, zone, there),
+            recv_sem=dkv_rsem.at[j],
+            device_id=at(row, zone, flip(lane, 2 if j == 2 else 1)),
             device_id_type=MESH,
         )
 
@@ -384,12 +388,14 @@
         lse_row = jnp.concatenate([st_in[there, r, 0:1, :] for r in range(head_total)], axis=1)
         delta_row = jnp.concatenate([st_in[there, r, 4:5, :] for r in range(head_total)], axis=1)
         query_sum = None
-        order = (0, 1, 2, 3) if s < 3 else (2, 3, 1, 0)
+        order = (0, 1, 2, 3) if s < 3 else (3, 2, 1, 0)
         for j in order:
             slot = flip(lane, j)
             if s == 0:
                 if j > 0:
                     kv_copy(j, slot).wait_recv()
+                if j == 2:
+                    launch(kv_pass())
                 kt_in[slot] = kv_in[slot, 0].T
             key = kv_in[slot, 0]
             value = kv_in[slot, 1]
@@ -406,13 +412,28 @@
             if s > 0:
                 key_term = dk_acc[slot] + key_term
                 value_term = dv_acc[slot] + value_term
-            if s == 3 and j > 0:
-                dkv_out[slot, 0] = key_term.astype(jnp.bfloat16)
-                dkv_out[slot, 1] = value_term.astype(jnp.bfloat16)
-                launch(dkv_copy(j, lane))
+            if s == 3 and j in (1, 3):
+                dkv_out[j, 0] = key_term.astype(jnp.bfloat16)
+                dkv_out[j, 1] = value_term.astype(jnp.bfloat16)
+                launch(dkv_copy(j))
             else:
                 dk_acc[slot] = key_term
                 dv_acc[slot] = value_term
+            if s == 3 and j == 1:
+                beside = flip(lane, 2)
+                dkv_copy(3).wait_recv()
+                key_pair = dk_acc[beside] + dkv_in[3, 0].astype(jnp.float32)
+                value_pair = dv_acc[beside] + dkv_in[3, 1].astype(jnp.float32)
+                dkv_out[2, 0] = key_pair.astype(jnp.bfloat16)
+                dkv_out[2, 1] = value_pair.astype(jnp.bfloat16)
+                launch(dkv_copy(2))
+            if s == 0 and j == 0:
+
+                @pl.when(inner)
+                def _():
+                    for r in rows_of(3):
+                        qd_copy(3, r, zone, row).start()
+
         query_low = query_sum.astype(jnp.bfloat16)
         block = q_ref.shape[0]
         for r in range(head_total):
@@ -433,11 +454,10 @@
 
     key_sum = dk_acc[lane]
     value_sum = dv_acc[lane]
-    for j in (1, 2, 3):
-        slot = flip(lane, j)
-        dkv_copy(j, slot).wait_recv()
-        key_sum = key_sum + dkv_in[slot, 0].astype(jnp.float32)
-        value_sum = value_sum + dkv_in[slot, 1].astype(jnp.float32)
+    for j in (1, 2):
+        dkv_copy(j).wait_recv()
+        key_sum = key_sum + dkv_in[j, 0].astype(jnp.float32)
+        value_sum = value_sum + dkv_in[j, 1].astype(jnp.float32)
     dk_ref[...] = (key_sum * scaling).astype(jnp.bfloat16)
     dv_ref[...] = value_sum.astype(jnp.bfloat16)
     for copy in sends:
@@ -450,13 +470,17 @@
             relay_copy(r).wait_send()
 
 
-def write_kernel(dq_ref, dk_ref, dv_ref, dq_out, dk_out, dv_out, sems):
-    pairs = ((dq_ref, dq_out), (dk_ref, dk_out), (dv_ref, dv_out))
-    copies = [pltpu.make_async_copy(src, dst, sems.at[i]) for i, (src, dst) in enumerate(pairs)]
-    for copy in copies:
-        copy.start()
-    for copy in copies:
-        copy.wait()
+def write_kernel(dq_ref, dk_ref, dv_ref, dq_out, dk_out, dv_out, dq_held, dk_held, dv_held, sems):
+    groups = ((dq_ref, dq_held, dq_out), (dk_ref, dk_held, dk_out), (dv_ref, dv_held, dv_out))
+    loads = [pltpu.make_async_copy(g[0], g[1], sems.at[0, i]) for i, g in enumerate(groups)]
+    stores = [pltpu.make_async_copy(g[1], g[2], sems.at[1, i]) for i, g in enumerate(groups)]
+    for load in loads:
+        load.start()
+    for load, store in zip(loads, stores):
+        load.wait()
+        store.start()
+    for store in stores:
+        store.wait()
 
 
 def fused_device(queries, keys, values, outputs, d_out, lse):
@@ -518,7 +542,7 @@
         out_shape=tuple(jax.ShapeDtypeStruct(x.shape, x.dtype) for x in results),
         in_specs=[hbm] * 3,
         out_specs=(hbm, hbm, hbm),
-        scratch_shapes=[dma((3,))],
+        scratch_shapes=[pltpu.VMEM(x.shape, x.dtype) for x in results] + [dma((2, 3))],
         compiler_params=pltpu.CompilerParams(vmem_limit_bytes=63 * 1024 * 1024),
     )(*results)
 

time: 35.1 us -> 27.8 us (0.79)
  Pallas kernels: 34.2 us -> 27 us
    pallas_call x1, Pallas kernels: 7.09 us -> 1.58 us  [fused_device(): pl.pallas_call(write_kernel, out_shape=tuple((jax.ShapeDtypeStruct(x.shap...]
    pallas_call x1, Pallas kernels: 27.1 us -> 25.4 us  [fused_device(): pl.pallas_call(functools.partial(fused_kernel, head_total), out_shape=(ja...]
where the time goes in v4:
time: 27.8 us; the launch traced here: 27.6 us
  Pallas kernels  27 us (97%)
  between operations  0.64 us (2%)
    pallas_call x1, Pallas kernels, fused_device(): pl.pallas_call(functools.partial(fused_kernel, head_total), out_shape=(ja...  25.4 us
    pallas_call x1, Pallas kernels, fused_device(): pl.pallas_call(write_kernel, out_shape=tuple((jax.ShapeDtypeStruct(x.shap...  1.58 us

profile of v4, /device:TPU:0, one launch (start us, length us, event | category | flops | bytes accessed | tf_op | source)
XLA Modules:
  0.0 27.6 jit_solution(7729426711230800303)
XLA Ops:
  0.6 25.4 %shard_map.85 = (bf16[128,256]{1,0:T(8,128)(2,1)}, bf16[256,128]{1,0:T(8,128)(2,1)}, bf16[256,128]{1,0:T(8,128)(2,1)}) custom-call(bf16[128,256]{1,0:T(8,128)(2,1)} %q_ref.1, bf16[256,128]{1,0:T(8,128)(2,1)} %k_ref.1, bf16[256,128]{1,0:T(8,128)(2,1)} %v_ref.1, bf16[128,256]{1,0:T(8,128)(2,1)} %o_ref.1, bf16[128,256]{1,0:T(8,128)(2,1)} %g_ref.1, f32[2,128]{1,0:T(2,128)} %lse_ref.1), custom_call_target="tpu_custom_call" | custom-call | flops 1342177280 | bytes 589824 | tf_op jit(solution)/shard_map/pallas_call | solution.py:496
  26.1 1.6 %shard_map.86 = (bf16[128,256]{1,0:T(8,128)(2,1)}, bf16[256,128]{1,0:T(8,128)(2,1)}, bf16[256,128]{1,0:T(8,128)(2,1)}) custom-call(bf16[128,256]{1,0:T(8,128)(2,1)} %get-tuple-element.6.dq_ref, bf16[256,128]{1,0:T(8,128)(2,1)} %get-tuple-element.7.dk_ref, bf16[256,128]{1,0:T(8,128)(2,1)} %get-tuple-element.8.dv_ref), custom_call_target="tpu_custom_call" | custom-call | tf_op jit(solution)/shard_map/pallas_call | solution.py:540

commit v5 on v4

--- a/solution.py
+++ b/solution.py
@@ -219,92 +219,73 @@
     zone = col // 4
     lane = lax.rem(col, 4)
     inner = lax.rem(zone + 1, 4) // 2 == 1
-    other = 1 - row
     dim = k_ref.shape[1]
+    block = q_ref.shape[0]
     scaling = dim ** (-0.5)
     MESH = pl.DeviceIdType.MESH
-
-    def at(r, z, m):
-        return (r, z * 4 + m)
+    bf16, f32 = jnp.bfloat16, jnp.float32
+    rows = (row, 1 - row)
+    steps = (0, 2, 1, 3)
+
+    def at(k, s, j):
+        return (rows[k], flip(zone, s) * 4 + flip(lane, j))
+
+    def rows_of(s):
+        return (1,) if s == 0 else (0, 1)
 
     loads = []
-    for h in range(head_total):
-        cols = pl.ds(h * dim, dim)
-        loads.append(pltpu.make_async_copy(q_ref.at[:, cols], qd_out.at[h, 0], in_sem.at[2 * h]))
-        loads.append(pltpu.make_async_copy(g_ref.at[:, cols], qd_out.at[h, 1], in_sem.at[2 * h + 1]))
+    row_loads = [pltpu.make_async_copy(lse_ref, lse_in, in_sem.at[8])]
+    for k in range(head_total):
+        cols = pl.ds(pl.multiple_of(rows[k] * dim, dim), dim)
+        loads.append(pltpu.make_async_copy(q_ref.at[:, cols], qd_out.at[k, 0], in_sem.at[k]))
+        loads.append(pltpu.make_async_copy(g_ref.at[:, cols], qd_out.at[k, 1], in_sem.at[2 + k]))
+        row_loads.append(pltpu.make_async_copy(o_ref.at[:, cols], o_in.at[k], in_sem.at[4 + k]))
     key_loads = [
-        pltpu.make_async_copy(k_ref, kv_in.at[lane, 0], in_sem.at[4]),
-        pltpu.make_async_copy(v_ref, kv_in.at[lane, 1], in_sem.at[5]),
-    ]
-    row_loads = [
-        pltpu.make_async_copy(o_ref, o_in, in_sem.at[6]),
-        pltpu.make_async_copy(lse_ref, lse_in, in_sem.at[7]),
+        pltpu.make_async_copy(k_ref, kv_in.at[0, 0], in_sem.at[6]),
+        pltpu.make_async_copy(v_ref, kv_in.at[0, 1], in_sem.at[7]),
     ]
     for load in loads + key_loads + row_loads:
         load.start()
 
-    mates = [at(row, zone, flip(lane, j)) for j in (1, 2)]
-    owners = [at(other, zone, lane)]
-    for s in (1, 2, 3):
-        owners += [at(r, flip(zone, s), lane) for r in range(head_total)]
+    peers = [at(0, 0, 1), at(0, 0, 2)] + [at(k, s, 0) for s in steps for k in rows_of(s)]
     barrier = pltpu.get_barrier_semaphore()
-    for peer in mates + owners:
+    for peer in peers:
         pl.semaphore_signal(barrier, inc=1, device_id=peer, device_id_type=MESH)
 
-    def kv_copy(j, slot):
+    def remote(src, dst, ssem, rsem, peer):
         return pltpu.make_async_remote_copy(
-            src_ref=kv_in.at[lane],
-            dst_ref=kv_in.at[slot],
-            send_sem=kv_ssem.at[j],
-            recv_sem=kv_rsem.at[slot],
-            device_id=at(row, zone, flip(lane, j)),
+            src_ref=src,
+            dst_ref=dst,
+            send_sem=ssem,
+            recv_sem=rsem,
+            device_id=peer,
             device_id_type=MESH,
         )
 
-    def kv_pass():
-        slot = flip(lane, 2)
-        return pltpu.make_async_remote_copy(
-            src_ref=kv_in.at[slot],
-            dst_ref=kv_in.at[slot],
-            send_sem=kv_ssem.at[3],
-            recv_sem=kv_rsem.at[slot],
-            device_id=at(row, zone, flip(lane, 1)),
-            device_id_type=MESH,
+    def kv_copy(j):
+        if j == 3:
+            return remote(kv_in.at[2], kv_in.at[3], kv_ssem.at[3], kv_rsem.at[3], at(0, 0, 1))
+        return remote(kv_in.at[0], kv_in.at[j], kv_ssem.at[j], kv_rsem.at[j], at(0, 0, j))
+
+    def st_copy(s, k):
+        return remote(st_out.at[k], st_in.at[s, k], st_ssem.at[s, k], st_rsem.at[s, k], at(k, s, 0))
+
+    def qd_copy(s, k):
+        return remote(
+            qd_out.at[k], qd_in.at[s, :, k], qd_ssem.at[s, k], qd_rsem.at[s, k], at(k, s, 0)
         )
 
-    def st_copy(s, r, slot_zone, slot_row):
-        return pltpu.make_async_remote_copy(
-            src_ref=st_out.at[r],
-            dst_ref=st_in.at[slot_zone, slot_row],
-            send_sem=st_ssem.at[s, r],
-            recv_sem=st_rsem.at[slot_zone, slot_row],
-            device_id=at(r, flip(zone, s), lane),
-            device_id_type=MESH,
+    def relay_copy(k):
+        return remote(
+            qd_in.at[2, :, k], qd_in.at[3, :, k], relay_ssem.at[k], qd_rsem.at[3, k], at(0, 1, 0)
         )
 
-    def qd_copy(s, r, slot_zone, slot_row):
-        return pltpu.make_async_remote_copy(
-            src_ref=qd_out.at[r],
-            dst_ref=qd_in.at[slot_zone, :, slot_row],
-            send_sem=qd_ssem.at[s, r],
-            recv_sem=qd_rsem.at[slot_zone, slot_row],
-            device_id=at(r, flip(zone, s), lane),
-            device_id_type=MESH,
-        )
-
-    def relay_copy(r):
-        slot_zone = flip(zone, 2)
-        return pltpu.make_async_remote_copy(
-            src_ref=qd_in.at[slot_zone, :, r],
-            dst_ref=qd_in.at[slot_zone, :, r],
-            send_sem=relay_ssem.at[r],
-            recv_sem=qd_rsem.at[slot_zone, r],
-            device_id=at(row, flip(zone, 1), lane),
-            device_id_type=MESH,
-        )
-
-    def rows_of(s):
-        return [other] if s == 0 else list(range(head_total))
+    def dq_copy(s, k):
+        return remote(dq_out.at[s, k], dq_in.at[s, k], dq_ssem.at[s, k], dq_rsem.at[s, k], at(k, s, 0))
+
+    def dkv_copy(j):
+        peer = at(0, 0, 2 if j == 2 else 1)
+        return remote(dkv_out.at[j], dkv_in.at[j], dkv_ssem.at[j], dkv_rsem.at[j], peer)
 
     sends = []
 
@@ -314,160 +295,130 @@
 
     for load in loads:
         load.wait()
-    pl.semaphore_wait(barrier, len(mates) + len(owners))
-    for r in rows_of(2):
-        launch(qd_copy(2, r, zone, row))
+    pl.semaphore_wait(barrier, len(peers))
+    for k in rows_of(2):
+        launch(qd_copy(2, k))
     for load in key_loads:
         load.wait()
     for j in (2, 1):
-        launch(kv_copy(j, lane))
+        launch(kv_copy(j))
     for s in (0, 1):
-        for r in rows_of(s):
-            launch(qd_copy(s, r, zone, row))
-    qd_in[zone, 0, row] = qd_out[row, 0]
-    qd_in[zone, 1, row] = qd_out[row, 1]
+        for k in rows_of(s):
+            launch(qd_copy(s, k))
+    qd_in[0, 0, 0] = qd_out[0, 0]
+    qd_in[0, 1, 0] = qd_out[0, 1]
 
     for load in row_loads:
         load.wait()
-    for h in range(head_total):
-        cols = slice(h * dim, (h + 1) * dim)
-        product = qd_out[h, 1].astype(jnp.float32) * o_in[:, cols].astype(jnp.float32)
+    for k in range(head_total):
+        product = qd_out[k, 1].astype(f32) * o_in[k].astype(f32)
         delta = lax.dot_general(
-            jnp.ones((8, dim), jnp.float32),
+            jnp.ones((8, dim), f32),
             product,
             (((1,), (1,)), ((), ())),
             precision=lax.Precision.HIGHEST,
-            preferred_element_type=jnp.float32,
+            preferred_element_type=f32,
         )
-        lse_rows = jnp.broadcast_to(lse_in[h : h + 1, :] * LOG2E, delta.shape)
+        lse_row = jnp.where(rows[k] == 0, lse_in[0:1, :], lse_in[1:2, :]) * LOG2E
         upper = lax.broadcasted_iota(jnp.int32, delta.shape, 0) < 4
-        st_out[h] = jnp.where(upper, lse_rows, delta)
-    st_in[zone, row] = st_out[row]
+        st_out[k] = jnp.where(upper, jnp.broadcast_to(lse_row, delta.shape), delta)
+    st_in[0, 0] = st_out[0]
     for s in (2, 0, 3, 1):
-        for r in rows_of(s):
-            launch(st_copy(s, r, zone, row))
-
-    def dq_copy(s, r, slot_row, slot_zone):
-        there = flip(zone, s)
-        return pltpu.make_async_remote_copy(
-            src_ref=dq_out.at[there, r],
-            dst_ref=dq_in.at[slot_row, slot_zone],
-            send_sem=dq_ssem.at[s, r],
-            recv_sem=dq_rsem.at[slot_row, slot_zone],
-            device_id=at(r, there, lane),
-            device_id_type=MESH,
-        )
-
-    def dkv_copy(j):
-        return pltpu.make_async_remote_copy(
-            src_ref=dkv_out.at[j],
-            dst_ref=dkv_in.at[j],
-            send_sem=dkv_ssem.at[j],
-            recv_sem=dkv_rsem.at[j],
-            device_id=at(row, zone, flip(lane, 2 if j == 2 else 1)),
-            device_id_type=MESH,
-        )
-
-    steps = (0, 2, 1, 3)
+        for k in rows_of(s):
+            launch(st_copy(s, k))
+
     for s in steps:
-        there = flip(zone, s)
-        for r in rows_of(s):
-            qd_copy(s, r, there, r).wait_recv()
+        for k in rows_of(s):
+            qd_copy(s, k).wait_recv()
         if s == 2:
 
             @pl.when(inner)
             def _():
-                for r in rows_of(2):
-                    relay_copy(r).start()
-
-        for r in rows_of(s):
-            st_copy(s, r, there, r).wait_recv()
-        rows2 = head_total * q_ref.shape[0]
-        query = qd_in[there, 0].reshape(rows2, dim)
-        grad = qd_in[there, 1].reshape(rows2, dim)
-        lse_row = jnp.concatenate([st_in[there, r, 0:1, :] for r in range(head_total)], axis=1)
-        delta_row = jnp.concatenate([st_in[there, r, 4:5, :] for r in range(head_total)], axis=1)
+                for k in rows_of(2):
+                    relay_copy(k).start()
+
+        for k in rows_of(s):
+            st_copy(s, k).wait_recv()
+        query = qd_in[s, 0].reshape(head_total * block, dim)
+        grad = qd_in[s, 1].reshape(head_total * block, dim)
+        query_t = query.T
+        grad_t = grad.T
+        lse_row = jnp.concatenate([st_in[s, k, 0:1, :] for k in range(head_total)], axis=1)
+        delta_row = jnp.concatenate([st_in[s, k, 4:5, :] for k in range(head_total)], axis=1)
         query_sum = None
         order = (0, 1, 2, 3) if s < 3 else (3, 2, 1, 0)
         for j in order:
-            slot = flip(lane, j)
             if s == 0:
                 if j > 0:
-                    kv_copy(j, slot).wait_recv()
+                    kv_copy(j).wait_recv()
                 if j == 2:
-                    launch(kv_pass())
-                kt_in[slot] = kv_in[slot, 0].T
-            key = kv_in[slot, 0]
-            value = kv_in[slot, 1]
-            dims = (((1,), (1,)), ((), ()))
-            scores = lax.dot_general(key, query, dims, preferred_element_type=jnp.float32)
-            grad_probs = lax.dot_general(value, grad, dims, preferred_element_type=jnp.float32)
+                    launch(kv_copy(3))
+                kt_in[j] = kv_in[j, 0].T
+            scores = jnp.dot(kv_in[j, 0], query_t, preferred_element_type=f32)
+            grad_probs = jnp.dot(kv_in[j, 1], grad_t, preferred_element_type=f32)
             probs = jnp.exp2(scores * (scaling * LOG2E) - lse_row)
-            probs_low = probs.astype(jnp.bfloat16)
-            grad_scores = (probs * (grad_probs - delta_row)).astype(jnp.bfloat16)
-            value_term = jnp.dot(probs_low, grad, preferred_element_type=jnp.float32)
-            key_term = jnp.dot(grad_scores, query, preferred_element_type=jnp.float32)
-            query_term = jnp.dot(kt_in[slot], grad_scores, preferred_element_type=jnp.float32)
+            probs_low = probs.astype(bf16)
+            grad_scores = (probs * (grad_probs - delta_row)).astype(bf16)
+            value_term = jnp.dot(probs_low, grad, preferred_element_type=f32)
+            key_term = jnp.dot(grad_scores, query, preferred_element_type=f32)
+            query_term = jnp.dot(kt_in[j], grad_scores, preferred_element_type=f32)
             query_sum = query_term if query_sum is None else query_sum + query_term
             if s > 0:
-                key_term = dk_acc[slot] + key_term
-                value_term = dv_acc[slot] + value_term
+                key_term = dk_acc[j] + key_term
+                value_term = dv_acc[j] + value_term
             if s == 3 and j in (1, 3):
-                dkv_out[j, 0] = key_term.astype(jnp.bfloat16)
-                dkv_out[j, 1] = value_term.astype(jnp.bfloat16)
+                dkv_out[j, 0] = key_term.astype(bf16)
+                dkv_out[j, 1] = value_term.astype(bf16)
                 launch(dkv_copy(j))
             else:
-                dk_acc[slot] = key_term
-                dv_acc[slot] = value_term
+                dk_acc[j] = key_term
+                dv_acc[j] = value_term
             if s == 3 and j == 1:
-                beside = flip(lane, 2)
                 dkv_copy(3).wait_recv()
-                key_pair = dk_acc[beside] + dkv_in[3, 0].astype(jnp.float32)
-                value_pair = dv_acc[beside] + dkv_in[3, 1].astype(jnp.float32)
-                dkv_out[2, 0] = key_pair.astype(jnp.bfloat16)
-                dkv_out[2, 1] = value_pair.astype(jnp.bfloat16)
+                dkv_out[2, 0] = (dk_acc[2] + dkv_in[3, 0].astype(f32)).astype(bf16)
+                dkv_out[2, 1] = (dv_acc[2] + dkv_in[3, 1].astype(f32)).astype(bf16)
                 launch(dkv_copy(2))
             if s == 0 and j == 0:
 
                 @pl.when(inner)
                 def _():
-                    for r in rows_of(3):
-                        qd_copy(3, r, zone, row).start()
-
-        query_low = query_sum.astype(jnp.bfloat16)
-        block = q_ref.shape[0]
-        for r in range(head_total):
-            dq_out[there, r] = query_low[:, r * block : (r + 1) * block]
-        if s == 0:
-            dq_in[row, zone] = dq_out[zone, row]
-        for r in rows_of(s):
-            launch(dq_copy(s, r, row, zone))
+                    for k in rows_of(3):
+                        qd_copy(3, k).start()
+
+        query_low = query_sum.astype(bf16)
+        for k in range(head_total):
+            dq_out[s, k] = query_low[:, k * block : (k + 1) * block]
+        for k in rows_of(s):
+            launch(dq_copy(s, k))
 
     for s in steps:
-        for r in rows_of(s):
-            dq_copy(s, r, r, flip(zone, s)).wait_recv()
-    for h in range(head_total):
-        total = dq_in[h, 0].astype(jnp.float32)
-        for z in range(1, 4):
-            total = total + dq_in[h, z].astype(jnp.float32)
-        dq_ref[:, h * dim : (h + 1) * dim] = (total * scaling).T.astype(jnp.bfloat16)
-
-    key_sum = dk_acc[lane]
-    value_sum = dv_acc[lane]
+        for k in rows_of(s):
+            dq_copy(s, k).wait_recv()
+    totals = []
+    for k in range(head_total):
+        total = (dq_out[0, 0] if k == 0 else dq_in[0, k]).astype(f32)
+        for s in (1, 2, 3):
+            total = total + dq_in[s, k].astype(f32)
+        totals.append((total * scaling).T)
+    dq_ref[:, :dim] = jnp.where(row == 0, totals[0], totals[1]).astype(bf16)
+    dq_ref[:, dim:] = jnp.where(row == 0, totals[1], totals[0]).astype(bf16)
+
+    key_sum = dk_acc[0]
+    value_sum = dv_acc[0]
     for j in (1, 2):
         dkv_copy(j).wait_recv()
-        key_sum = key_sum + dkv_in[j, 0].astype(jnp.float32)
-        value_sum = value_sum + dkv_in[j, 1].astype(jnp.float32)
-    dk_ref[...] = (key_sum * scaling).astype(jnp.bfloat16)
-    dv_ref[...] = value_sum.astype(jnp.bfloat16)
+        key_sum = key_sum + dkv_in[j, 0].astype(f32)
+        value_sum = value_sum + dkv_in[j, 1].astype(f32)
+    dk_ref[...] = (key_sum * scaling).astype(bf16)
+    dv_ref[...] = value_sum.astype(bf16)
     for copy in sends:
         copy.wait_send()
 
     @pl.when(inner)
     def _():
-        for r in rows_of(3):
-            qd_copy(3, r, zone, row).wait_send()
-            relay_copy(r).wait_send()
+        for k in rows_of(3):
+            qd_copy(3, k).wait_send()
+            relay_copy(k).wait_send()
 
 
 def write_kernel(dq_ref, dk_ref, dv_ref, dq_out, dk_out, dv_out, dq_held, dk_held, dv_held, sems):
@@ -512,7 +463,7 @@
             pltpu.VMEM((lanes, key_rows, dim), f32),
             pltpu.VMEM((lanes, key_rows, dim), f32),
             pltpu.VMEM((zones, head_total, dim, block), bf16),
-            pltpu.VMEM((head_total, zones, dim, block), bf16),
+            pltpu.VMEM((zones, head_total, dim, block), bf16),
             pltpu.VMEM((lanes, 2, key_rows, dim), bf16),
             pltpu.VMEM((lanes, 2, key_rows, dim), bf16),
             dma((zones, head_total)),
@@ -522,12 +473,12 @@
             dma((lanes,)),
             dma((lanes,)),
             dma((zones, head_total)),
-            dma((head_total, zones)),
+            dma((zones, head_total)),
             dma((lanes,)),
             dma((lanes,)),
-            pltpu.VMEM(outputs.shape, bf16),
+            pltpu.VMEM((head_total, block, dim), bf16),
             pltpu.VMEM(lse.shape, f32),
-            dma((8,)),
+            dma((9,)),
             dma((head_total,)),
         ],
         compiler_params=pltpu.CompilerParams(

time: 27.8 us -> 28.7 us (1.032)
  Pallas kernels: 27 us -> 27.9 us
    pallas_call x1, Pallas kernels: 25.4 us -> 26.3 us  [fused_device(): pl.pallas_call(functools.partial(fused_kernel, head_total), out_shape=(ja...]
where the time goes in v5:
time: 28.7 us; the launch traced here: 28.5 us
  Pallas kernels  27.9 us (97%)
  between operations  0.64 us (2%)
    pallas_call x1, Pallas kernels, fused_device(): pl.pallas_call(functools.partial(fused_kernel, head_total), out_shape=(ja...  26.3 us
    pallas_call x1, Pallas kernels, fused_device(): pl.pallas_call(write_kernel, out_shape=tuple((jax.ShapeDtypeStruct(x.shap...  1.58 us

profile of v5, /device:TPU:0, one launch (start us, length us, event | category | flops | bytes accessed | tf_op | source)
XLA Modules:
  0.0 28.5 jit_solution(5417315265819306417)
XLA Ops:
  0.6 26.3 %shard_map.85 = (bf16[128,256]{1,0:T(8,128)(2,1)}, bf16[256,128]{1,0:T(8,128)(2,1)}, bf16[256,128]{1,0:T(8,128)(2,1)}) custom-call(bf16[128,256]{1,0:T(8,128)(2,1)} %q_ref.1, bf16[256,128]{1,0:T(8,128)(2,1)} %k_ref.1, bf16[256,128]{1,0:T(8,128)(2,1)} %v_ref.1, bf16[128,256]{1,0:T(8,128)(2,1)} %o_ref.1, bf16[128,256]{1,0:T(8,128)(2,1)} %g_ref.1, f32[2,128]{1,0:T(2,128)} %lse_ref.1), custom_call_target="tpu_custom_call" | custom-call | flops 1342177280 | bytes 589824 | tf_op jit(solution)/shard_map/pallas_call | solution.py:447
  26.9 1.6 %shard_map.86 = (bf16[128,256]{1,0:T(8,128)(2,1)}, bf16[256,128]{1,0:T(8,128)(2,1)}, bf16[256,128]{1,0:T(8,128)(2,1)}) custom-call(bf16[128,256]{1,0:T(8,128)(2,1)} %get-tuple-element.6.dq_ref, bf16[256,128]{1,0:T(8,128)(2,1)} %get-tuple-element.7.dk_ref, bf16[256,128]{1,0:T(8,128)(2,1)} %get-tuple-element.8.dv_ref), custom_call_target="tpu_custom_call" | custom-call | tf_op jit(solution)/shard_map/pallas_call | solution.py:491

commit v6 on v5

--- a/solution.py
+++ b/solution.py
@@ -184,9 +184,9 @@
     o_ref,
     g_ref,
     lse_ref,
-    dq_ref,
-    dk_ref,
-    dv_ref,
+    dq_in,
+    dkv_in,
+    own_out,
     qd_out,
     qd_in,
     st_out,
@@ -196,9 +196,8 @@
     dk_acc,
     dv_acc,
     dq_out,
-    dq_in,
     dkv_out,
-    dkv_in,
+    pair_in,
     qd_ssem,
     qd_rsem,
     st_ssem,
@@ -281,11 +280,12 @@
         )
 
     def dq_copy(s, k):
-        return remote(dq_out.at[s, k], dq_in.at[s, k], dq_ssem.at[s, k], dq_rsem.at[s, k], at(k, s, 0))
+        return remote(dq_out.at[s, k], dq_in.at[s, row], dq_ssem.at[s, k], dq_rsem.at[s, k], at(k, s, 0))
 
     def dkv_copy(j):
         peer = at(0, 0, 2 if j == 2 else 1)
-        return remote(dkv_out.at[j], dkv_in.at[j], dkv_ssem.at[j], dkv_rsem.at[j], peer)
+        target = pair_in if j == 3 else dkv_in.at[j - 1]
+        return remote(dkv_out.at[j], target, dkv_ssem.at[j], dkv_rsem.at[j], peer)
 
     sends = []
 
@@ -341,8 +341,6 @@
             st_copy(s, k).wait_recv()
         query = qd_in[s, 0].reshape(head_total * block, dim)
         grad = qd_in[s, 1].reshape(head_total * block, dim)
-        query_t = query.T
-        grad_t = grad.T
         lse_row = jnp.concatenate([st_in[s, k, 0:1, :] for k in range(head_total)], axis=1)
         delta_row = jnp.concatenate([st_in[s, k, 4:5, :] for k in range(head_total)], axis=1)
         query_sum = None
@@ -354,8 +352,9 @@
                 if j == 2:
                     launch(kv_copy(3))
                 kt_in[j] = kv_in[j, 0].T
-            scores = jnp.dot(kv_in[j, 0], query_t, preferred_element_type=f32)
-            grad_probs = jnp.dot(kv_in[j, 1], grad_t, preferred_element_type=f32)
+            dims = (((1,), (1,)), ((), ()))
+            scores = lax.dot_general(kv_in[j, 0], query, dims, preferred_element_type=f32)
+            grad_probs = lax.dot_general(kv_in[j, 1], grad, dims, preferred_element_type=f32)
             probs = jnp.exp2(scores * (scaling * LOG2E) - lse_row)
             probs_low = probs.astype(bf16)
             grad_scores = (probs * (grad_probs - delta_row)).astype(bf16)
@@ -375,8 +374,8 @@
                 dv_acc[j] = value_term
             if s == 3 and j == 1:
                 dkv_copy(3).wait_recv()
-                dkv_out[2, 0] = (dk_acc[2] + dkv_in[3, 0].astype(f32)).astype(bf16)
-                dkv_out[2, 1] = (dv_acc[2] + dkv_in[3, 1].astype(f32)).astype(bf16)
+                dkv_out[2, 0] = (dk_acc[2] + pair_in[0].astype(f32)).astype(bf16)
+                dkv_out[2, 1] = (dv_acc[2] + pair_in[1].astype(f32)).astype(bf16)
                 launch(dkv_copy(2))
             if s == 0 and j == 0:
 
@@ -391,26 +390,20 @@
         for k in rows_of(s):
             launch(dq_copy(s, k))
 
+    own = [
+        pltpu.make_async_copy(dk_acc.at[0], own_out.at[0], in_sem.at[0]),
+        pltpu.make_async_copy(dv_acc.at[0], own_out.at[1], in_sem.at[1]),
+        pltpu.make_async_copy(dq_out.at[0, 0], dq_in.at[0, row], in_sem.at[2]),
+    ]
+    for copy in own:
+        copy.start()
     for s in steps:
         for k in rows_of(s):
             dq_copy(s, k).wait_recv()
-    totals = []
-    for k in range(head_total):
-        total = (dq_out[0, 0] if k == 0 else dq_in[0, k]).astype(f32)
-        for s in (1, 2, 3):
-            total = total + dq_in[s, k].astype(f32)
-        totals.append((total * scaling).T)
-    dq_ref[:, :dim] = jnp.where(row == 0, totals[0], totals[1]).astype(bf16)
-    dq_ref[:, dim:] = jnp.where(row == 0, totals[1], totals[0]).astype(bf16)
-
-    key_sum = dk_acc[0]
-    value_sum = dv_acc[0]
     for j in (1, 2):
         dkv_copy(j).wait_recv()
-        key_sum = key_sum + dkv_in[j, 0].astype(f32)
-        value_sum = value_sum + dkv_in[j, 1].astype(f32)
-    dk_ref[...] = (key_sum * scaling).astype(bf16)
-    dv_ref[...] = value_sum.astype(bf16)
+    for copy in own:
+        copy.wait()
     for copy in sends:
         copy.wait_send()
 
@@ -421,17 +414,19 @@
             relay_copy(k).wait_send()
 
 
-def write_kernel(dq_ref, dk_ref, dv_ref, dq_out, dk_out, dv_out, dq_held, dk_held, dv_held, sems):
-    groups = ((dq_ref, dq_held, dq_out), (dk_ref, dk_held, dk_out), (dv_ref, dv_held, dv_out))
-    loads = [pltpu.make_async_copy(g[0], g[1], sems.at[0, i]) for i, g in enumerate(groups)]
-    stores = [pltpu.make_async_copy(g[1], g[2], sems.at[1, i]) for i, g in enumerate(groups)]
-    for load in loads:
-        load.start()
-    for load, store in zip(loads, stores):
-        load.wait()
-        store.start()
-    for store in stores:
-        store.wait()
+def sum_kernel(dq_parts, dkv_parts, own, dq_ref, dk_ref, dv_ref):
+    bf16, f32 = jnp.bfloat16, jnp.float32
+    dim = own.shape[2]
+    scaling = dim ** (-0.5)
+    for h in range(dq_parts.shape[1]):
+        total = dq_parts[0, h].astype(f32)
+        for s in range(1, dq_parts.shape[0]):
+            total = total + dq_parts[s, h].astype(f32)
+        dq_ref[:, h * dim : (h + 1) * dim] = (total * scaling).T.astype(bf16)
+    key_sum = own[0] + dkv_parts[0, 0].astype(f32) + dkv_parts[1, 0].astype(f32)
+    value_sum = own[1] + dkv_parts[0, 1].astype(f32) + dkv_parts[1, 1].astype(f32)
+    dk_ref[...] = (key_sum * scaling).astype(bf16)
+    dv_ref[...] = value_sum.astype(bf16)
 
 
 def fused_device(queries, keys, values, outputs, d_out, lse):
@@ -447,12 +442,12 @@
     results = pl.pallas_call(
         functools.partial(fused_kernel, head_total),
         out_shape=(
-            jax.ShapeDtypeStruct(queries.shape, bf16),
-            jax.ShapeDtypeStruct(keys.shape, bf16),
-            jax.ShapeDtypeStruct(values.shape, bf16),
+            jax.ShapeDtypeStruct((zones, head_total, dim, block), bf16),
+            jax.ShapeDtypeStruct((2, 2, key_rows, dim), bf16),
+            jax.ShapeDtypeStruct((2, key_rows, dim), f32),
         ),
         in_specs=[hbm] * 6,
-        out_specs=(vmem, vmem, vmem),
+        out_specs=(hbm, hbm, hbm),
         scratch_shapes=[
             pltpu.VMEM((head_total, 2, block, dim), bf16),
             pltpu.VMEM((zones, 2, head_total, block, dim), bf16),
@@ -463,9 +458,8 @@
             pltpu.VMEM((lanes, key_rows, dim), f32),
             pltpu.VMEM((lanes, key_rows, dim), f32),
             pltpu.VMEM((zones, head_total, dim, block), bf16),
-            pltpu.VMEM((zones, head_total, dim, block), bf16),
             pltpu.VMEM((lanes, 2, key_rows, dim), bf16),
-            pltpu.VMEM((lanes, 2, key_rows, dim), bf16),
+            pltpu.VMEM((2, key_rows, dim), bf16),
             dma((zones, head_total)),
             dma((zones, head_total)),
             dma((zones, head_total)),
@@ -489,11 +483,10 @@
         ),
     )(queries, keys, values, outputs, d_out, lse)
     return pl.pallas_call(
-        write_kernel,
-        out_shape=tuple(jax.ShapeDtypeStruct(x.shape, x.dtype) for x in results),
-        in_specs=[hbm] * 3,
-        out_specs=(hbm, hbm, hbm),
-        scratch_shapes=[pltpu.VMEM(x.shape, x.dtype) for x in results] + [dma((2, 3))],
+        sum_kernel,
+        out_shape=tuple(jax.ShapeDtypeStruct(x.shape, bf16) for x in (queries, keys, values)),
+        in_specs=[vmem] * 3,
+        out_specs=(vmem, vmem, vmem),
         compiler_params=pltpu.CompilerParams(vmem_limit_bytes=63 * 1024 * 1024),
     )(*results)
 

time: 28.7 us -> 28.2 us (0.983)
  Pallas kernels: 27.9 us -> 27.4 us
    pallas_call x1, Pallas kernels: 26.3 us -> 25.5 us  [fused_device(): pl.pallas_call(functools.partial(fused_kernel, head_total), out_shape=(ja...]
where the time goes in v6:
time: 28.2 us; the launch traced here: 28 us
  Pallas kernels  27.4 us (97%)
  between operations  0.64 us (2%)
    pallas_call x1, Pallas kernels, fused_device(): pl.pallas_call(functools.partial(fused_kernel, head_total), out_shape=(ja...  25.5 us
    pallas_call x1, Pallas kernels, fused_device(): pl.pallas_call(sum_kernel, out_shape=tuple((jax.ShapeDtypeStruct(x.shape,...  1.86 us

profile of v6, /device:TPU:0, one launch (start us, length us, event | category | flops | bytes accessed | tf_op | source)
XLA Modules:
  0.0 28.0 jit_solution(4678566564743053723)
XLA Ops:
  0.6 25.5 %shard_map.85 = (bf16[4,2,128,128]{3,2,1,0:T(8,128)(2,1)}, bf16[2,2,256,128]{3,2,1,0:T(8,128)(2,1)}, f32[2,256,128]{2,1,0:T(8,128)}) custom-call(bf16[128,256]{1,0:T(8,128)(2,1)} %q_ref.1, bf16[256,128]{1,0:T(8,128)(2,1)} %k_ref.1, bf16[256,128]{1,0:T(8,128)(2,1)} %v_ref.1, bf16[128,256]{1,0:T(8,128)(2,1)} %o_ref.1, bf16[128,256]{1,0:T(8,128)(2,1)} %g_ref.1, ...), custom_call_target="tpu_custom_call" | custom-call | flops 1342177280 | bytes 589824 | tf_op jit(solution)/shard_map/pallas_call | solution.py:442
  26.2 1.9 %shard_map.86 = (bf16[128,256]{1,0:T(8,128)(2,1)}, bf16[256,128]{1,0:T(8,128)(2,1)}, bf16[256,128]{1,0:T(8,128)(2,1)}) custom-call(bf16[4,2,128,128]{3,2,1,0:T(8,128)(2,1)} %get-tuple-element.6.dq_parts, bf16[2,2,256,128]{3,2,1,0:T(8,128)(2,1)} %get-tuple-element.7.dkv_parts, f32[2,256,128]{2,1,0:T(8,128)} %get-tuple-element.8.own), custom_call_target="tpu_custom_call" | custom-call | tf_op jit(solution)/shard_map/pallas_call | solution.py:485

commit v7 on v6

--- a/solution.py
+++ b/solution.py
@@ -302,9 +302,7 @@
         load.wait()
     for j in (2, 1):
         launch(kv_copy(j))
-    for s in (0, 1):
-        for k in rows_of(s):
-            launch(qd_copy(s, k))
+    launch(qd_copy(0, 1))
     qd_in[0, 0, 0] = qd_out[0, 0]
     qd_in[0, 1, 0] = qd_out[0, 1]
 
@@ -328,15 +326,16 @@
             launch(st_copy(s, k))
 
     for s in steps:
-        for k in rows_of(s):
-            qd_copy(s, k).wait_recv()
         if s == 2:
 
-            @pl.when(inner)
+            @pl.when(jnp.logical_not(inner))
             def _():
                 for k in rows_of(2):
-                    relay_copy(k).start()
-
+                    qd_copy(2, k).wait_recv()
+
+        else:
+            for k in rows_of(s):
+                qd_copy(s, k).wait_recv()
         for k in rows_of(s):
             st_copy(s, k).wait_recv()
         query = qd_in[s, 0].reshape(head_total * block, dim)
@@ -351,6 +350,15 @@
                     kv_copy(j).wait_recv()
                 if j == 2:
                     launch(kv_copy(3))
+
+                    @pl.when(inner)
+                    def _():
+                        for k in rows_of(3):
+                            qd_copy(3, k).start()
+                        for k in rows_of(2):
+                            qd_copy(2, k).wait_recv()
+                            relay_copy(k).start()
+
                 kt_in[j] = kv_in[j, 0].T
             dims = (((1,), (1,)), ((), ()))
             scores = lax.dot_general(kv_in[j, 0], query, dims, preferred_element_type=f32)
@@ -372,24 +380,19 @@
             else:
                 dk_acc[j] = key_term
                 dv_acc[j] = value_term
-            if s == 3 and j == 1:
-                dkv_copy(3).wait_recv()
-                dkv_out[2, 0] = (dk_acc[2] + pair_in[0].astype(f32)).astype(bf16)
-                dkv_out[2, 1] = (dv_acc[2] + pair_in[1].astype(f32)).astype(bf16)
-                launch(dkv_copy(2))
             if s == 0 and j == 0:
-
-                @pl.when(inner)
-                def _():
-                    for k in rows_of(3):
-                        qd_copy(3, k).start()
-
+                for k in rows_of(1):
+                    launch(qd_copy(1, k))
         query_low = query_sum.astype(bf16)
         for k in range(head_total):
             dq_out[s, k] = query_low[:, k * block : (k + 1) * block]
         for k in rows_of(s):
             launch(dq_copy(s, k))
 
+    dkv_copy(3).wait_recv()
+    dkv_out[2, 0] = (dk_acc[2] + pair_in[0].astype(f32)).astype(bf16)
+    dkv_out[2, 1] = (dv_acc[2] + pair_in[1].astype(f32)).astype(bf16)
+    launch(dkv_copy(2))
     own = [
         pltpu.make_async_copy(dk_acc.at[0], own_out.at[0], in_sem.at[0]),
         pltpu.make_async_copy(dv_acc.at[0], own_out.at[1], in_sem.at[1]),

time: 28.2 us -> 31.2 us (1.11)
  Pallas kernels: 27.4 us -> 30.4 us
    pallas_call x1, Pallas kernels: 25.5 us -> 28.5 us  [fused_device(): pl.pallas_call(functools.partial(fused_kernel, head_total), out_shape=(ja...]
where the time goes in v7:
time: 31.2 us; the launch traced here: 31 us
  Pallas kernels  30.4 us (97%)
  between operations  0.64 us (2%)
    pallas_call x1, Pallas kernels, fused_device(): pl.pallas_call(functools.partial(fused_kernel, head_total), out_shape=(ja...  28.5 us
    pallas_call x1, Pallas kernels, fused_device(): pl.pallas_call(sum_kernel, out_shape=tuple((jax.ShapeDtypeStruct(x.shape,...  1.86 us

profile of v7, /device:TPU:0, one launch (start us, length us, event | category | flops | bytes accessed | tf_op | source)
XLA Modules:
  0.0 31.0 jit_solution(5725624216225251098)
XLA Ops:
  0.6 28.5 %shard_map.85 = (bf16[4,2,128,128]{3,2,1,0:T(8,128)(2,1)}, bf16[2,2,256,128]{3,2,1,0:T(8,128)(2,1)}, f32[2,256,128]{2,1,0:T(8,128)}) custom-call(bf16[128,256]{1,0:T(8,128)(2,1)} %q_ref.1, bf16[256,128]{1,0:T(8,128)(2,1)} %k_ref.1, bf16[256,128]{1,0:T(8,128)(2,1)} %v_ref.1, bf16[128,256]{1,0:T(8,128)(2,1)} %o_ref.1, bf16[128,256]{1,0:T(8,128)(2,1)} %g_ref.1, ...), custom_call_target="tpu_custom_call" | custom-call | flops 1342177280 | bytes 589824 | tf_op jit(solution)/shard_map/pallas_call | solution.py:445
  29.2 1.9 %shard_map.86 = (bf16[128,256]{1,0:T(8,128)(2,1)}, bf16[256,128]{1,0:T(8,128)(2,1)}, bf16[256,128]{1,0:T(8,128)(2,1)}) custom-call(bf16[4,2,128,128]{3,2,1,0:T(8,128)(2,1)} %get-tuple-element.6.dq_parts, bf16[2,2,256,128]{3,2,1,0:T(8,128)(2,1)} %get-tuple-element.7.dkv_parts, f32[2,256,128]{2,1,0:T(8,128)} %get-tuple-element.8.own), custom_call_target="tpu_custom_call" | custom-call | tf_op jit(solution)/shard_map/pallas_call | solution.py:488

commit v8 on v4

--- a/solution.py
+++ b/solution.py
@@ -368,7 +368,7 @@
             device_id_type=MESH,
         )
 
-    steps = (0, 2, 1, 3)
+    steps = (0, 1, 2, 3)
     for s in steps:
         there = flip(zone, s)
         for r in rows_of(s):

time: 27.8 us -> 31.9 us (1.15)
  Pallas kernels: 27 us -> 31 us
    pallas_call x1, Pallas kernels: 25.4 us -> 29.4 us  [fused_device(): pl.pallas_call(functools.partial(fused_kernel, head_total), out_shape=(ja...]
where the time goes in v8:
time: 31.9 us; the launch traced here: 31.7 us
  Pallas kernels  31 us (97%)
  between operations  0.64 us (2%)
    pallas_call x1, Pallas kernels, fused_device(): pl.pallas_call(functools.partial(fused_kernel, head_total), out_shape=(ja...  29.4 us
    pallas_call x1, Pallas kernels, fused_device(): pl.pallas_call(write_kernel, out_shape=tuple((jax.ShapeDtypeStruct(x.shap...  1.58 us

profile of v8, /device:TPU:0, one launch (start us, length us, event | category | flops | bytes accessed | tf_op | source)
XLA Modules:
  0.0 31.7 jit_solution(13999365877153121218)
XLA Ops:
  0.6 29.4 %shard_map.85 = (bf16[128,256]{1,0:T(8,128)(2,1)}, bf16[256,128]{1,0:T(8,128)(2,1)}, bf16[256,128]{1,0:T(8,128)(2,1)}) custom-call(bf16[128,256]{1,0:T(8,128)(2,1)} %q_ref.1, bf16[256,128]{1,0:T(8,128)(2,1)} %k_ref.1, bf16[256,128]{1,0:T(8,128)(2,1)} %v_ref.1, bf16[128,256]{1,0:T(8,128)(2,1)} %o_ref.1, bf16[128,256]{1,0:T(8,128)(2,1)} %g_ref.1, f32[2,128]{1,0:T(2,128)} %lse_ref.1), custom_call_target="tpu_custom_call" | custom-call | flops 1342177280 | bytes 589824 | tf_op jit(solution)/shard_map/pallas_call | solution.py:496
  30.1 1.6 %shard_map.86 = (bf16[128,256]{1,0:T(8,128)(2,1)}, bf16[256,128]{1,0:T(8,128)(2,1)}, bf16[256,128]{1,0:T(8,128)(2,1)}) custom-call(bf16[128,256]{1,0:T(8,128)(2,1)} %get-tuple-element.6.dq_ref, bf16[256,128]{1,0:T(8,128)(2,1)} %get-tuple-element.7.dk_ref, bf16[256,128]{1,0:T(8,128)(2,1)} %get-tuple-element.8.dv_ref), custom_call_target="tpu_custom_call" | custom-call | tf_op jit(solution)/shard_map/pallas_call | solution.py:540

commit v9 on v8

--- a/solution.py
+++ b/solution.py
@@ -212,7 +212,6 @@
     o_in,
     lse_in,
     in_sem,
-    relay_ssem,
 ):
     row = lax.axis_index("row")
     col = lax.axis_index("col")
@@ -292,17 +291,6 @@
             device_id_type=MESH,
         )
 
-    def relay_copy(r):
-        slot_zone = flip(zone, 2)
-        return pltpu.make_async_remote_copy(
-            src_ref=qd_in.at[slot_zone, :, r],
-            dst_ref=qd_in.at[slot_zone, :, r],
-            send_sem=relay_ssem.at[r],
-            recv_sem=qd_rsem.at[slot_zone, r],
-            device_id=at(row, flip(zone, 1), lane),
-            device_id_type=MESH,
-        )
-
     def rows_of(s):
         return [other] if s == 0 else list(range(head_total))
 
@@ -315,6 +303,11 @@
     for load in loads:
         load.wait()
     pl.semaphore_wait(barrier, len(mates) + len(owners))
+    @pl.when(jnp.logical_not(inner))
+    def _():
+        for r in rows_of(3):
+            qd_copy(3, r, zone, row).start()
+
     for r in rows_of(2):
         launch(qd_copy(2, r, zone, row))
     for load in key_loads:
@@ -373,13 +366,6 @@
         there = flip(zone, s)
         for r in rows_of(s):
             qd_copy(s, r, there, r).wait_recv()
-        if s == 2:
-
-            @pl.when(inner)
-            def _():
-                for r in rows_of(2):
-                    relay_copy(r).start()
-
         for r in rows_of(s):
             st_copy(s, r, there, r).wait_recv()
         rows2 = head_total * q_ref.shape[0]
@@ -462,12 +448,8 @@
     dv_ref[...] = value_sum.astype(jnp.bfloat16)
     for copy in sends:
         copy.wait_send()
-
-    @pl.when(inner)
-    def _():
-        for r in rows_of(3):
-            qd_copy(3, r, zone, row).wait_send()
-            relay_copy(r).wait_send()
+    for r in rows_of(3):
+        qd_copy(3, r, zone, row).wait_send()
 
 
 def write_kernel(dq_ref, dk_ref, dv_ref, dq_out, dk_out, dv_out, dq_held, dk_held, dv_held, sems):
@@ -528,7 +510,6 @@
             pltpu.VMEM(outputs.shape, bf16),
             pltpu.VMEM(lse.shape, f32),
             dma((8,)),
-            dma((head_total,)),
         ],
         compiler_params=pltpu.CompilerParams(
             collective_id=0, has_side_effects=True, vmem_limit_bytes=63 * 1024 * 1024

time: 31.9 us -> 29.1 us (0.912)
  Pallas kernels: 31 us -> 28.3 us
    pallas_call x1, Pallas kernels: 29.4 us -> 26.7 us  [fused_device(): pl.pallas_call(functools.partial(fused_kernel, head_total), out_shape=(ja...]
where the time goes in v9:
time: 29.1 us; the launch traced here: 28.9 us
  Pallas kernels  28.3 us (97%)
  between operations  0.64 us (2%)
    pallas_call x1, Pallas kernels, fused_device(): pl.pallas_call(functools.partial(fused_kernel, head_total), out_shape=(ja...  26.7 us
    pallas_call x1, Pallas kernels, fused_device(): pl.pallas_call(write_kernel, out_shape=tuple((jax.ShapeDtypeStruct(x.shap...  1.58 us

profile of v9, /device:TPU:0, one launch (start us, length us, event | category | flops | bytes accessed | tf_op | source)
XLA Modules:
  0.0 28.9 jit_solution(4403581312321648691)
XLA Ops:
  0.6 26.7 %shard_map.85 = (bf16[128,256]{1,0:T(8,128)(2,1)}, bf16[256,128]{1,0:T(8,128)(2,1)}, bf16[256,128]{1,0:T(8,128)(2,1)}) custom-call(bf16[128,256]{1,0:T(8,128)(2,1)} %q_ref.1, bf16[256,128]{1,0:T(8,128)(2,1)} %k_ref.1, bf16[256,128]{1,0:T(8,128)(2,1)} %v_ref.1, bf16[128,256]{1,0:T(8,128)(2,1)} %o_ref.1, bf16[128,256]{1,0:T(8,128)(2,1)} %g_ref.1, f32[2,128]{1,0:T(2,128)} %lse_ref.1), custom_call_target="tpu_custom_call" | custom-call | flops 1342177280 | bytes 589824 | tf_op jit(solution)/shard_map/pallas_call | solution.py:478
  27.4 1.6 %shard_map.86 = (bf16[128,256]{1,0:T(8,128)(2,1)}, bf16[256,128]{1,0:T(8,128)(2,1)}, bf16[256,128]{1,0:T(8,128)(2,1)}) custom-call(bf16[128,256]{1,0:T(8,128)(2,1)} %get-tuple-element.6.dq_ref, bf16[256,128]{1,0:T(8,128)(2,1)} %get-tuple-element.7.dk_ref, bf16[256,128]{1,0:T(8,128)(2,1)} %get-tuple-element.8.dv_ref), custom_call_target="tpu_custom_call" | custom-call | tf_op jit(solution)/shard_map/pallas_call | solution.py:521

commit v10 on v4

--- a/solution.py
+++ b/solution.py
@@ -315,15 +315,15 @@
     for load in loads:
         load.wait()
     pl.semaphore_wait(barrier, len(mates) + len(owners))
-    for r in rows_of(2):
-        launch(qd_copy(2, r, zone, row))
+    for s in (2, 1):
+        for r in rows_of(s):
+            launch(qd_copy(s, r, zone, row))
     for load in key_loads:
         load.wait()
     for j in (2, 1):
         launch(kv_copy(j, lane))
-    for s in (0, 1):
-        for r in rows_of(s):
-            launch(qd_copy(s, r, zone, row))
+    for r in rows_of(0):
+        launch(qd_copy(0, r, zone, row))
     qd_in[zone, 0, row] = qd_out[row, 0]
     qd_in[zone, 1, row] = qd_out[row, 1]
 
@@ -371,15 +371,16 @@
     steps = (0, 2, 1, 3)
     for s in steps:
         there = flip(zone, s)
-        for r in rows_of(s):
-            qd_copy(s, r, there, r).wait_recv()
         if s == 2:
 
-            @pl.when(inner)
+            @pl.when(jnp.logical_not(inner))
             def _():
                 for r in rows_of(2):
-                    relay_copy(r).start()
-
+                    qd_copy(2, r, flip(zone, 2), r).wait_recv()
+
+        else:
+            for r in rows_of(s):
+                qd_copy(s, r, there, r).wait_recv()
         for r in rows_of(s):
             st_copy(s, r, there, r).wait_recv()
         rows2 = head_total * q_ref.shape[0]
@@ -396,6 +397,13 @@
                     kv_copy(j, slot).wait_recv()
                 if j == 2:
                     launch(kv_pass())
+
+                    @pl.when(inner)
+                    def _():
+                        for r in rows_of(2):
+                            qd_copy(2, r, flip(zone, 2), r).wait_recv()
+                            relay_copy(r).start()
+
                 kt_in[slot] = kv_in[slot, 0].T
             key = kv_in[slot, 0]
             value = kv_in[slot, 1]

time: 27.8 us -> 27.9 us (level)
  no operation moved by 1% of the time
where the time goes in v10:
time: 27.9 us; the launch traced here: 27.6 us
  Pallas kernels  27 us (97%)
  between operations  0.64 us (2%)
    pallas_call x1, Pallas kernels, fused_device(): pl.pallas_call(functools.partial(fused_kernel, head_total), out_shape=(ja...  25.4 us
    pallas_call x1, Pallas kernels, fused_device(): pl.pallas_call(write_kernel, out_shape=tuple((jax.ShapeDtypeStruct(x.shap...  1.58 us

profile of v10, /device:TPU:0, one launch (start us, length us, event | category | flops | bytes accessed | tf_op | source)
XLA Modules:
  0.0 27.6 jit_solution(12447856167838262273)
XLA Ops:
  0.6 25.4 %shard_map.85 = (bf16[128,256]{1,0:T(8,128)(2,1)}, bf16[256,128]{1,0:T(8,128)(2,1)}, bf16[256,128]{1,0:T(8,128)(2,1)}) custom-call(bf16[128,256]{1,0:T(8,128)(2,1)} %q_ref.1, bf16[256,128]{1,0:T(8,128)(2,1)} %k_ref.1, bf16[256,128]{1,0:T(8,128)(2,1)} %v_ref.1, bf16[128,256]{1,0:T(8,128)(2,1)} %o_ref.1, bf16[128,256]{1,0:T(8,128)(2,1)} %g_ref.1, f32[2,128]{1,0:T(2,128)} %lse_ref.1), custom_call_target="tpu_custom_call" | custom-call | flops 1342177280 | bytes 589824 | tf_op jit(solution)/shard_map/pallas_call | solution.py:504
  26.1 1.6 %shard_map.86 = (bf16[128,256]{1,0:T(8,128)(2,1)}, bf16[256,128]{1,0:T(8,128)(2,1)}, bf16[256,128]{1,0:T(8,128)(2,1)}) custom-call(bf16[128,256]{1,0:T(8,128)(2,1)} %get-tuple-element.6.dq_ref, bf16[256,128]{1,0:T(8,128)(2,1)} %get-tuple-element.7.dk_ref, bf16[256,128]{1,0:T(8,128)(2,1)} %get-tuple-element.8.dv_ref), custom_call_target="tpu_custom_call" | custom-call | tf_op jit(solution)/shard_map/pallas_call | solution.py:548
